TPU v7x, 32 devices: a whole 2x2x4 slice. The times are simulated.
32 devices in a mesh: gx: 16 (over z, y, core), gy: 2 (over x).
Axes of the slice: x: 2, y: 2, z: 4, core: 2. Of those that a mesh axis runs over, the one named last changes fastest.
Arguments:
- velocity: float32 [3, 262144], P(None, ('gx', 'gy')), may hold values from -6 to 6
- inv_mass: float32 [262144], P(('gx', 'gy')), may hold values from 0.5 to 2
- drag: float32 [262144], P(('gx', 'gy')), may hold values from 0.2 to 5
- grain_cell: int32 [262144], P(('gx', 'gy')), may hold values from 0 to 2047
- boundary_list: int32 [16384], P(('gx', 'gy')), may hold values from 0 to 8191
- contact_pair: int32 [2, 524288], P(None, ('gx', 'gy')), may hold values from 0 to 10239, as said below
- frames: float32 [9, 524288], P(None, ('gx', 'gy')), may hold values from -0.45 to 1.4
- blocks: float32 [9, 524288], P(None, ('gx', 'gy')), may hold values from -0.15 to 1
- impulse_start: float32 [3, 524288], P(None, ('gx', 'gy')), may hold values from -4 to 4
- gap: float32 [3, 524288], P(None, ('gx', 'gy')), may hold values from -4 to 4
- contact_mask: int32 [524288], P(('gx', 'gy')), may hold values 0 or 1
- pressure: float32 [8, 256, 32], P(None, 'gx', 'gy'), may hold values from -6 to 6
Outputs:
- final_velocity: float32 [3, 262144], P(None, ('gx', 'gy'))
- final_impulse: float32 [3, 524288], P(None, ('gx', 'gy'))
Inputs may be any that keep to these rules, and one draw needn't show every extreme that they name: `contact_pair`: slots below 8192 are the block's own grains, slots from 8192 on are the four ghost groups of 512. Contacts are sorted in space: for the contacts of tile t of a block (contacts 128 t to 128 t + 127), a slot below 8192 lies in (64 t + r) mod 8192 and a slot from 8192 on in 8192 + ((16 t + r) mod 4 * 512), with r from 0 to 255 and from 0 to 63 respectively.
All inputs are finite; a program needn't handle non-finite values. No bound on the sum of `contact_mask` on one device may be relied on, other than what follows from the above.
Results may differ from a plain program's by a relative error of at most 0.0003.
Values sent between devices are 32-bit elements; how exact they have to be, the bound alone decides.
A program may use at most 64 MiB of HBM per device.

v0:
```python
import jax
import jax.numpy as jnp
from jax import lax
from jax.experimental import pallas as pl
from jax.experimental.pallas import tpu as pltpu
from jax.sharding import PartitionSpec as P

SWEEPS = 2
TIME_STEP = 0.5
FRICTION = 0.5
FLOOR_VALUE = 0.1
LANES = 128
ROWS = 32
STAGE = 48
F32 = jnp.float32
BF16 = jnp.bfloat16


def take_lanes(values, lanes):
    return jnp.take_along_axis(values, lanes, axis=1, mode="promise_in_bounds")


def spread_row(ref, row):
    return jnp.broadcast_to(ref[pl.ds(row, 1), :], (8, LANES))


def step_kernel(
    sizes,
    vel_hbm, mass_hbm, drag_hbm, cell_hbm, bound_hbm, pair_hbm, frame_hbm, block_hbm,
    start_hbm, gap_hbm, mask_hbm, pres_hbm,
    out_vel, out_imp,
    vel_ref, mass_ref, drag_ref, cell_ref, bound_ref, pair_ref, frame_ref, block_ref,
    start_ref, gap_ref, mask_ref, pres_raw, pres_wide, pres_ref,
    pres_in, ghost_in, sum_in, ghost_out, sum_out,
    slope_s, vel_s, free_s, stage, ends, codes, lanes_s, table, ext, ghost_s,
    left, sums, bound_hot, bound_row,
    send_sem, recv_sem, load_sem,
):
    nx, ny = sizes
    tiles = mask_ref.shape[0]
    own_rows = mass_ref.shape[0]
    side_rows = bound_ref.shape[0]
    ghost_rows = 4 * side_rows
    cell_rows = pres_ref.shape[0]
    ext_rows = 2 * own_rows + 8
    gpad = ghost_rows + 8
    pairs = tiles // 2
    row_iota = lax.broadcasted_iota(jnp.int32, (8, LANES), 0)

    mx, my = lax.axis_index("gx"), lax.axis_index("gy")
    sides = (
        (lax.rem(mx + nx - 1, nx), my),
        (lax.rem(mx + 1, nx), my),
        (mx, lax.rem(my + ny - 1, ny)),
        (mx, lax.rem(my + 1, ny)),
    )

    loads = [
        pltpu.make_async_copy(source, target, load_sem.at[k])
        for k, (source, target) in enumerate(
            (
                (pair_hbm, pair_ref), (frame_hbm, frame_ref), (block_hbm, block_ref),
                (start_hbm, start_ref), (gap_hbm, gap_ref), (vel_hbm, vel_ref),
                (bound_hbm, bound_ref), (cell_hbm, cell_ref), (drag_hbm, drag_ref),
                (mass_hbm, mass_ref), (mask_hbm, mask_ref),
            )
        )
    ]
    pres_load = pltpu.make_async_copy(pres_hbm, pres_raw, load_sem.at[11])
    pres_load.start()
    for load in loads:
        load.start()

    barrier = pltpu.get_barrier_semaphore()
    for side in sides:
        pl.semaphore_signal(barrier, inc=1, device_id=side, device_id_type=pl.DeviceIdType.MESH)

    lane = lax.broadcasted_iota(jnp.int32, (cell_rows, LANES), 1)
    pres_load.wait()
    width = pres_raw.shape[2]
    pres_wide[:, 0:width] = pres_raw[...].reshape(-1, width)
    per_row = LANES // width
    p = pres_wide[pl.ds(0, cell_rows, stride=per_row), :]
    for k in range(1, per_row):
        piece = pltpu.roll(pres_wide[pl.ds(k, cell_rows, stride=per_row), :], k * width, 1)
        p = jnp.where(lane < k * width, p, piece)
    pres_ref[...] = p
    pl.semaphore_wait(barrier, 4)

    def exchange(step, source, target):
        copies = []
        for g in range(4):
            copies.append(
                pltpu.make_async_remote_copy(
                    src_ref=source(g),
                    dst_ref=target(g ^ 1),
                    send_sem=send_sem.at[step, g],
                    recv_sem=recv_sem.at[step, g ^ 1],
                    device_id=sides[g],
                    device_id_type=pl.DeviceIdType.MESH,
                )
            )
        for copy in copies:
            copy.start()
        return copies

    def finish(copies):
        for copy in copies:
            copy.wait()

    flying = exchange(0, lambda g: pres_ref, lambda g: pres_in.at[g])

    for load in loads:
        load.wait()

    def stage_tile(t, carry):
        cols = pl.ds(pl.multiple_of(t * LANES, LANES), LANES)
        base = pl.multiple_of(t * STAGE, 8)
        stage[pl.ds(base, 9), :] = frame_ref[:, cols]
        stage[pl.ds(base + 16, 9), :] = block_ref[:, cols]
        stage[pl.ds(base + 32, 3), :] = start_ref[:, cols]
        stage[pl.ds(base + 40, 3), :] = gap_ref[:, cols]
        ends[pl.ds(pl.multiple_of(t * 8, 8), 2), :] = pair_ref[:, cols]
        return carry

    lax.fori_loop(0, tiles, stage_tile, 0, unroll=4)

    def stage_grain(t, carry):
        cols = pl.ds(pl.multiple_of(t * LANES, LANES), LANES)
        vel_s[pl.ds(pl.multiple_of(t * 8, 8), 3), :] = vel_ref[:, cols]
        return carry

    lax.fori_loop(0, own_rows, stage_grain, 0, unroll=4)

    def place(u, carry):
        tile = u * 8 + row_iota
        for e in range(2):
            slot = ends[pl.ds(u * 64 + 1 - e, 8, stride=8), :]
            row = slot >> 7
            own = (row - (tile >> 1)) & (own_rows - 1)
            far = 3 + ((row - own_rows - (tile >> 3)) & (ghost_rows - 1))
            at = pl.ds(pl.multiple_of(e * tiles + u * 8, 8), 8)
            codes[at, :] = jnp.where(row < own_rows, own, far)
            lanes_s[at, :] = slot & (LANES - 1)
        return carry

    lax.fori_loop(0, tiles // 8, place, 0, unroll=2)

    bound_all = bound_ref[...]
    bound_lane = bound_all & (LANES - 1)
    bound_at = bound_all >> 7
    hot_iota = lax.broadcasted_iota(jnp.int32, (LANES, LANES), 0)
    row_hot = lax.broadcasted_iota(jnp.int32, (own_rows, LANES), 0)
    for q in range(side_rows):
        cols = slice(q * LANES, (q + 1) * LANES)
        bound_hot[:, cols] = jnp.where(hot_iota == bound_lane[q : q + 1], 1.0, 0.0).astype(BF16)
        bound_row[:, cols] = jnp.where(row_hot == bound_at[q : q + 1], 1.0, 0.0).astype(BF16)
    two_lane = jnp.concatenate([bound_lane, bound_lane], axis=0)
    two_at = jnp.concatenate([bound_at, bound_at], axis=0)
    half = own_rows // 2
    upper = row_iota < side_rows

    def pick_bound():
        def body(k, acc):
            acc = list(acc)
            for i in range(4):
                r = k * 4 + i
                hit = two_at == jnp.where(upper, r, r + half)
                for c in range(3):
                    low = spread_row(ext, c * ext_rows + 2 * r)
                    high = spread_row(ext, c * ext_rows + 2 * (r + half))
                    got = take_lanes(jnp.where(upper, low, high), two_lane)
                    acc[c] = jnp.where(hit, got, acc[c])
            return tuple(acc)

        zero = jnp.zeros((8, LANES), F32)
        acc = lax.fori_loop(0, half // 4, body, (zero, zero, zero), unroll=4)
        low_at = two_at < half
        for c in range(3):
            got = acc[c]
            ghost_out[c * side_rows : (c + 1) * side_rows, :] = jnp.where(
                low_at[:side_rows], got[:side_rows], got[side_rows:]
            )

    def spread_current(c, value):
        ext[pl.ds(c * ext_rows, own_rows, stride=2), :] = value
        ext[pl.ds(c * ext_rows + 1, own_rows, stride=2), :] = value
        ext[pl.ds(c * ext_rows + 2 * own_rows, 8), :] = ext[pl.ds(c * ext_rows, 8), :]

    finish(flying)

    even = (lax.broadcasted_iota(jnp.int32, (cell_rows, LANES), 0) & 1) == 0
    up1 = lambda a: jnp.concatenate([a[1:], a[:1]], axis=0)
    down1 = lambda a: jnp.concatenate([a[-1:], a[:-1]], axis=0)
    turn = lambda a, n: pltpu.roll(a, n % LANES, 1)
    p_next = turn(p, -16)
    plus = jnp.where(lane < 112, p_next, jnp.where(even, up1(p_next), down1(turn(pres_in[1], -16))))
    p_prev = turn(p, 16)
    minus = jnp.where(lane >= 16, p_prev, jnp.where(even, up1(turn(pres_in[0], 16)), down1(p_prev)))
    slope_s[0:cell_rows] = (plus - minus) * 0.5
    plus = jnp.where((lane & 15) < 15, turn(p, -1), turn(pres_in[3], 15))
    minus = jnp.where((lane & 15) > 0, turn(p, 1), turn(pres_in[2], -15))
    slope_s[cell_rows : 2 * cell_rows] = (plus - minus) * 0.5
    none = jnp.zeros((2, LANES), F32)
    slope_s[2 * cell_rows : 3 * cell_rows] = (
        jnp.concatenate([p[2:], none], axis=0) - jnp.concatenate([none, p[:-2]], axis=0)
    ) * 0.5

    def free(k, carry):
        at = pl.ds(pl.multiple_of(k * 8, 8), 8)
        cells = cell_ref[at, :]
        cell_at, cell_lane = cells >> 7, cells & (LANES - 1)
        drag, mass = drag_ref[at, :], mass_ref[at, :]
        for c in range(3):
            slope = jnp.zeros((8, LANES), F32)
            for r in range(cell_rows):
                got = take_lanes(spread_row(slope_s, c * cell_rows + r), cell_lane)
                slope = jnp.where(cell_at == r, got, slope)
            v = vel_s[pl.ds(k * 64 + c, 8, stride=8), :]
            free_s[pl.ds(pl.multiple_of(c * own_rows + k * 8, 8), 8), :] = (
                v - TIME_STEP * (drag + mass) * slope
            ) / (1.0 + TIME_STEP * drag)
        return carry

    lax.fori_loop(0, own_rows // 8, free, 0, unroll=2)
    for c in range(3):
        spread_current(c, free_s[c * own_rows : (c + 1) * own_rows, :])
    pick_bound()
    flying = exchange(1, lambda g: ghost_out, lambda g: ghost_in.at[0, g])

    iotas = [
        (lax.broadcasted_iota(jnp.int32, (16, LANES), 0) + 16 * q).astype(F32).astype(BF16)
        for q in range(8)
    ]
    one, zero16 = jnp.ones((16, LANES), BF16), jnp.zeros((16, LANES), BF16)

    def build(t, carry):
        for e in range(2):
            row = lanes_s[pl.ds(e * tiles + t, 1), :].astype(F32)
            row = jnp.broadcast_to(row, (16, LANES)).astype(BF16)
            for q in range(8):
                table[
                    pl.ds(pl.multiple_of(t * LANES + 16 * q, 16), 16), e * LANES : (e + 1) * LANES
                ] = jnp.where(iotas[q] == row, one, zero16)
        return carry

    lax.fori_loop(0, tiles, build, 0, unroll=2)
    for i in range(16):
        left[i * ROWS + 24 : (i + 1) * ROWS, :] = jnp.zeros((8, LANES), F32)

    nt = (((1,), (1,)), ((), ()))
    for sweep in range(SWEEPS):
        finish(flying)
        for c in range(3):
            for g in range(4):
                ghost_s[c * gpad + g * side_rows : c * gpad + (g + 1) * side_rows, :] = ghost_in[
                    sweep, g, c * side_rows : (c + 1) * side_rows, :
                ]
            ghost_s[c * gpad + ghost_rows : c * gpad + ghost_rows + 1, :] = ghost_in[
                sweep, 0, c * side_rows : c * side_rows + 1, :
            ]

        def contacts(u, carry):
            at = pl.ds(pl.multiple_of(u * 8, 8), 8)
            code, lanes = [], []
            for e in range(2):
                end_at = pl.ds(pl.multiple_of(e * tiles + u * 8, 8), 8)
                code.append(codes[end_at, :])
                lanes.append(lanes_s[end_at, :])
            relative = []
            for c in range(3):
                own = [ext[pl.ds(c * ext_rows + u * 8 + 2 * h, 8), :] for h in range(3)]
                own += [spread_row(ghost_s, c * gpad + u + h) for h in range(2)]
                ends_val = []
                for e in range(2):
                    val = take_lanes(own[4], lanes[e])
                    for h in range(3, -1, -1):
                        val = jnp.where(code[e] == h, take_lanes(own[h], lanes[e]), val)
                    ends_val.append(val)
                relative.append(ends_val[0] - ends_val[1])
            part = lambda k: stage[pl.ds(u * (8 * STAGE) + k, 8, stride=STAGE), :]
            fr = [part(k) for k in range(9)]
            target = [
                fr[3 * m] * relative[0]
                + fr[3 * m + 1] * relative[1]
                + fr[3 * m + 2] * relative[2]
                + part(40 + m)
                for m in range(3)
            ]
            trial = []
            for k in range(3):
                before = part(32 + k) if sweep == 0 else out_imp[k, at, :]
                trial.append(
                    before
                    - (
                        part(16 + 3 * k) * target[0]
                        + part(17 + 3 * k) * target[1]
                        + part(18 + 3 * k) * target[2]
                    )
                )
            active = mask_ref[at, :].astype(F32)
            normal = jnp.maximum(trial[0], 0.0)
            tangent = jnp.sqrt(trial[1] * trial[1] + trial[2] * trial[2])
            factor = jnp.minimum(1.0, FRICTION * normal / jnp.maximum(tangent, FLOOR_VALUE))
            imp = [normal * active, factor * trial[1] * active, factor * trial[2] * active]
            for k in range(3):
                out_imp[k, at, :] = imp[k]
            for c in range(3):
                push = fr[c] * imp[0] + fr[3 + c] * imp[1] + fr[6 + c] * imp[2]
                high = push.astype(BF16).astype(F32)
                for s, term in enumerate((high, push - high)):
                    for e in range(2):
                        signed = term if e == 0 else -term
                        for h in range(5):
                            left[
                                pl.ds(e * 8 * ROWS + (h * 3 + c) * 2 + s, 8, stride=ROWS), :
                            ] = jnp.where(code[e] == h, signed, 0.0)
            for q in range(4):
                total = None
                for i in (2 * q, 2 * q + 1):
                    got = lax.dot_general(
                        jnp.concatenate(
                            [
                                left[i * ROWS : (i + 1) * ROWS, :].astype(BF16),
                                left[(i + 8) * ROWS : (i + 9) * ROWS, :].astype(BF16),
                            ],
                            axis=1,
                        ),
                        table[pl.ds(pl.multiple_of((u * 8 + i) * LANES, LANES), LANES), :],
                        nt,
                        preferred_element_type=F32,
                    )
                    total = got if total is None else total + got
                sums[pl.ds(pl.multiple_of((u * 4 + q + 4) * ROWS, ROWS), ROWS), :] = total
            return carry

        lax.fori_loop(0, tiles // 8, contacts, 0, unroll=8)
        sums[0 : 4 * ROWS, :] = sums[pairs * ROWS : (pairs + 4) * ROWS, :]

        for c in range(3):
            for r in range(0, ghost_rows, 8):
                total = None
                for h in range(2):
                    for q in range(4):
                        for s in range(2):
                            first = (4 * (r - h) + q + 4) * ROWS + ((3 + h) * 3 + c) * 2 + s
                            got = sums[pl.ds(first, 8, stride=4 * ROWS), :]
                            total = got if total is None else total + got
                for i in range(0, 8, side_rows):
                    sum_out[
                        (r + i) // side_rows, c * side_rows : (c + 1) * side_rows, :
                    ] = total[i : i + side_rows]
        flying = exchange(2 + 2 * sweep, lambda g: sum_out.at[g], lambda g: sum_in.at[sweep, g])
        own_total = []
        for c in range(3):
            parts = []
            for r in range(0, own_rows, 8):
                total = None
                for h in range(3):
                    for s in range(2):
                        first = (r - h + 4) * ROWS + (h * 3 + c) * 2 + s
                        got = sums[pl.ds(first, 8, stride=ROWS), :]
                        total = got if total is None else total + got
                parts.append(total)
            own_total.append(jnp.concatenate(parts, axis=0))
        finish(flying)
        received = (
            sum_in[sweep, 0] + sum_in[sweep, 1] + sum_in[sweep, 2] + sum_in[sweep, 3]
        )
        high = received.astype(BF16).astype(F32)
        low = received - high
        mass = mass_ref[...]
        for c in range(3):
            total = own_total[c]
            for term in (high, low):
                row = jnp.concatenate(
                    [
                        bound_row[:, q * LANES : (q + 1) * LANES]
                        * jnp.broadcast_to(
                            term[c * side_rows + q : c * side_rows + q + 1], (own_rows, LANES)
                        ).astype(BF16)
                        for q in range(side_rows)
                    ],
                    axis=1,
                )
                total = total + lax.dot_general(
                    row, bound_hot[...], nt, preferred_element_type=F32
                )
            current = free_s[c * own_rows : (c + 1) * own_rows, :] + mass * total
            if sweep < SWEEPS - 1:
                spread_current(c, current)
            else:
                out_vel[c] = current
        if sweep < SWEEPS - 1:
            pick_bound()
            flying = exchange(
                3 + 2 * sweep, lambda g: ghost_out, lambda g: ghost_in.at[sweep + 1, g]
            )


def solution(mesh):
    sizes = (mesh.shape["gx"], mesh.shape["gy"])

    def local(
        velocity, inv_mass, drag, grain_cell, boundary_list, contact_pair, frames, blocks,
        impulse_start, gap, contact_mask, pressure,
    ):
        own_rows = velocity.shape[1] // LANES
        tiles = contact_pair.shape[1] // LANES
        side_rows = boundary_list.shape[0] // LANES
        cell_rows = pressure.size // LANES
        gpad = 4 * side_rows + 8
        rounds = 1 + 2 * SWEEPS
        vmem = pl.BlockSpec(memory_space=pltpu.VMEM)
        out_vel, out_imp = pl.pallas_call(
            lambda *refs: step_kernel(sizes, *refs),
            out_shape=(
                jax.ShapeDtypeStruct((3, own_rows, LANES), F32),
                jax.ShapeDtypeStruct((3, tiles, LANES), F32),
            ),
            in_specs=[pl.BlockSpec(memory_space=pltpu.HBM)] * 12,
            out_specs=(vmem, vmem),
            scratch_shapes=[
                pltpu.VMEM((3, velocity.shape[1]), F32),
                pltpu.VMEM((own_rows, LANES), F32),
                pltpu.VMEM((own_rows, LANES), F32),
                pltpu.VMEM((own_rows, LANES), jnp.int32),
                pltpu.VMEM((side_rows, LANES), jnp.int32),
                pltpu.VMEM((2, contact_pair.shape[1]), jnp.int32),
                pltpu.VMEM((9, contact_pair.shape[1]), F32),
                pltpu.VMEM((9, contact_pair.shape[1]), F32),
                pltpu.VMEM((3, contact_pair.shape[1]), F32),
                pltpu.VMEM((3, contact_pair.shape[1]), F32),
                pltpu.VMEM((tiles, LANES), jnp.int32),
                pltpu.VMEM(pressure.shape, F32),
                pltpu.VMEM((pressure.size // pressure.shape[2], LANES), F32),
                pltpu.VMEM((cell_rows, LANES), F32),
                pltpu.VMEM((4, cell_rows, LANES), F32),
                pltpu.VMEM((SWEEPS, 4, 3 * side_rows, LANES), F32),
                pltpu.VMEM((SWEEPS, 4, 3 * side_rows, LANES), F32),
                pltpu.VMEM((3 * side_rows, LANES), F32),
                pltpu.VMEM((4, 3 * side_rows, LANES), F32),
                pltpu.VMEM((3 * cell_rows, LANES), F32),
                pltpu.VMEM((own_rows * 8, LANES), F32),
                pltpu.VMEM((3 * own_rows, LANES), F32),
                pltpu.VMEM((tiles * STAGE, LANES), F32),
                pltpu.VMEM((tiles * 8, LANES), jnp.int32),
                pltpu.VMEM((2 * tiles, LANES), jnp.int32),
                pltpu.VMEM((2 * tiles, LANES), jnp.int32),
                pltpu.VMEM((tiles * LANES, 2 * LANES), BF16),
                pltpu.VMEM((3 * (2 * own_rows + 8), LANES), F32),
                pltpu.VMEM((3 * gpad, LANES), F32),
                pltpu.VMEM((16 * ROWS, LANES), F32),
                pltpu.VMEM(((tiles // 2 + 4) * ROWS, LANES), F32),
                pltpu.VMEM((LANES, side_rows * LANES), BF16),
                pltpu.VMEM((own_rows, side_rows * LANES), BF16),
                pltpu.SemaphoreType.DMA((rounds, 4)),
                pltpu.SemaphoreType.DMA((rounds, 4)),
                pltpu.SemaphoreType.DMA((12,)),
            ],
            compiler_params=pltpu.CompilerParams(
                collective_id=0, has_side_effects=True, vmem_limit_bytes=62 * 1024 * 1024
            ),
        )(
            velocity,
            inv_mass.reshape(own_rows, LANES),
            drag.reshape(own_rows, LANES),
            grain_cell.reshape(own_rows, LANES),
            boundary_list.reshape(side_rows, LANES),
            contact_pair,
            frames,
            blocks,
            impulse_start,
            gap,
            contact_mask.reshape(tiles, LANES),
            pressure,
        )
        return out_vel.reshape(3, -1), out_imp.reshape(3, -1)

    grains, lists = P(("gx", "gy")), P(None, ("gx", "gy"))
    return jax.shard_map(
        local,
        mesh=mesh,
        in_specs=(
            lists, grains, grains, grains, grains, lists, lists, lists, lists, lists, grains,
            P(None, "gx", "gy"),
        ),
        out_specs=(lists, lists),
        check_vma=False,
    )
```

profile of v0, /device:TPU:0, one launch (start us, length us, event | category | flops | bytes accessed | tf_op | source)
XLA Modules:
  0.0 40.6 jit_solution(12914973895536729768)
XLA Ops:
  0.6 37.4 %shard_map.131 = (f32[3,64,128]{2,1,0:T(8,128)}, f32[3,128,128]{2,1,0:T(8,128)}) custom-call(f32[3,8192]{1,0:T(4,128)} %refs_0_.1, f32[64,128]{1,0:T(8,128)} %bitcast.18, f32[64,128]{1,0:T(8,128)} %bitcast.19, s32[64,128]{1,0:T(8,128)} %bitcast.20, s32[4,128]{1,0:T(4,128)} %bitcast.21, s32[2,16384]{1,0:T(2,128)} %refs_5_.1, f32[9,16384]{1,0:T(8,128)} %refs_6_.1, ...), custom_call_target="tpu_custom_call" | custom-call | tf_op jit(solution)/shard_map/pallas_call | solution.py:415
  38.0 0.0 copy-start
  38.1 1.8 %copy.18 = f32[1,3,128,128]{3,1,2,0:T(4,128)} copy(f32[1,3,128,128]{3,2,1,0:T(8,128)} %bitcast.14) | data formatting | bytes 393216
  39.9 0.0 copy-done
  39.9 0.7 %copy.19 = f32[1,3,64,128]{3,1,2,0:T(4,128)} copy(f32[1,3,64,128]{3,2,1,0:T(8,128)S(1)} %bitcast.16) | data formatting | bytes 196608
Async XLA Ops:
  38.0 1.8 %copy-start = (f32[3,64,128]{2,1,0:T(8,128)S(1)}, f32[3,64,128]{2,1,0:T(8,128)}, u32[]{:S(2)}) copy-start(f32[3,64,128]{2,1,0:T(8,128)} %get-tuple-element.4) | copy-start | bytes 294916
where the time goes:
time: 40.7 us; the launch traced here: 40.6 us
  Pallas kernels  37.4 us (92%)
  local copies, waits for them, and re-layouts  2.53 us (6%)
  between operations  0.65 us (2%)
    pallas_call x1, Pallas kernels, local(): pl.pallas_call(lambda *refs: step_kernel(sizes, *refs), out_shape=(jax.Sh...  37.4 us
    unnamed x4, local copies, waits for them, and re-layouts  2.53 us

commit v1 on v0

--- a/solution.py
+++ b/solution.py
@@ -10,8 +10,12 @@
 FRICTION = 0.5
 FLOOR_VALUE = 0.1
 LANES = 128
-ROWS = 32
-STAGE = 48
+HALF = LANES // 2
+ROWS = 48
+PITCH = 49
+STAGE = 49
+OWN_PITCH = 25
+GHOST_PITCH = 17
 F32 = jnp.float32
 BF16 = jnp.bfloat16
 
@@ -32,8 +36,8 @@
     vel_ref, mass_ref, drag_ref, cell_ref, bound_ref, pair_ref, frame_ref, block_ref,
     start_ref, gap_ref, mask_ref, pres_raw, pres_wide, pres_ref,
     pres_in, ghost_in, sum_in, ghost_out, sum_out,
-    slope_s, vel_s, free_s, stage, ends, codes, lanes_s, table, ext, ghost_s,
-    left, sums, bound_hot, bound_row,
+    slope_s, vel_s, free_s, stage, ends, codes, lanes_s, spots, table, ext, ghost_s,
+    left, sums, ghost_sums, bound_hot, bound_row,
     send_sem, recv_sem, load_sem,
 ):
     nx, ny = sizes
@@ -43,8 +47,11 @@
     ghost_rows = 4 * side_rows
     cell_rows = pres_ref.shape[0]
     ext_rows = 2 * own_rows + 8
-    gpad = ghost_rows + 8
-    pairs = tiles // 2
+    gpad = 2 * ghost_rows
+    own_slots = own_rows * LANES
+    ghost_slots = ghost_rows * LANES
+    own_part = own_rows + 2
+    ghost_part = ghost_rows + 1
     row_iota = lax.broadcasted_iota(jnp.int32, (8, LANES), 0)
 
     mx, my = lax.axis_index("gx"), lax.axis_index("gy")
@@ -104,9 +111,12 @@
             copy.start()
         return copies
 
+    sent = []
+
     def finish(copies):
         for copy in copies:
-            copy.wait()
+            copy.wait_recv()
+        sent.extend(copies)
 
     flying = exchange(0, lambda g: pres_ref, lambda g: pres_in.at[g])
 
@@ -115,19 +125,19 @@
 
     def stage_tile(t, carry):
         cols = pl.ds(pl.multiple_of(t * LANES, LANES), LANES)
-        base = pl.multiple_of(t * STAGE, 8)
+        base = t * STAGE
         stage[pl.ds(base, 9), :] = frame_ref[:, cols]
         stage[pl.ds(base + 16, 9), :] = block_ref[:, cols]
         stage[pl.ds(base + 32, 3), :] = start_ref[:, cols]
         stage[pl.ds(base + 40, 3), :] = gap_ref[:, cols]
-        ends[pl.ds(pl.multiple_of(t * 8, 8), 2), :] = pair_ref[:, cols]
+        ends[pl.ds(t * 3, 2), :] = pair_ref[:, cols]
         return carry
 
     lax.fori_loop(0, tiles, stage_tile, 0, unroll=4)
 
     def stage_grain(t, carry):
         cols = pl.ds(pl.multiple_of(t * LANES, LANES), LANES)
-        vel_s[pl.ds(pl.multiple_of(t * 8, 8), 3), :] = vel_ref[:, cols]
+        vel_s[pl.ds(t * 3, 3), :] = vel_ref[:, cols]
         return carry
 
     lax.fori_loop(0, own_rows, stage_grain, 0, unroll=4)
@@ -135,13 +145,15 @@
     def place(u, carry):
         tile = u * 8 + row_iota
         for e in range(2):
-            slot = ends[pl.ds(u * 64 + 1 - e, 8, stride=8), :]
-            row = slot >> 7
-            own = (row - (tile >> 1)) & (own_rows - 1)
-            far = 3 + ((row - own_rows - (tile >> 3)) & (ghost_rows - 1))
+            slot = ends[pl.ds(u * 24 + 1 - e, 8, stride=3), :]
+            own = slot < own_slots
+            near = (slot - HALF * tile) & (own_slots - 1)
+            far = (slot - own_slots - HALF * (tile >> 2)) & (ghost_slots - 1)
+            rel = jnp.where(own, near, far)
             at = pl.ds(pl.multiple_of(e * tiles + u * 8, 8), 8)
-            codes[at, :] = jnp.where(row < own_rows, own, far)
-            lanes_s[at, :] = slot & (LANES - 1)
+            codes[at, :] = jnp.where(own, 0, 4) + (rel >> 6)
+            lanes_s[at, :] = rel & (LANES - 1)
+            spots[at, :] = (rel & (HALF - 1)).astype(F32)
         return carry
 
     lax.fori_loop(0, tiles // 8, place, 0, unroll=2)
@@ -160,7 +172,7 @@
     half = own_rows // 2
     upper = row_iota < side_rows
 
-    def pick_bound():
+    def pick_bound(turn):
         def body(k, acc):
             acc = list(acc)
             for i in range(4):
@@ -178,13 +190,20 @@
         low_at = two_at < half
         for c in range(3):
             got = acc[c]
-            ghost_out[c * side_rows : (c + 1) * side_rows, :] = jnp.where(
+            ghost_out[turn, c * side_rows : (c + 1) * side_rows, :] = jnp.where(
                 low_at[:side_rows], got[:side_rows], got[side_rows:]
             )
 
+    def spread_halves(ref, first, value):
+        rows = value.shape[0]
+        turned = pltpu.roll(value, HALF, 1)
+        after = jnp.concatenate([turned[1:], turned[:1]], axis=0)
+        first_half = lax.broadcasted_iota(jnp.int32, value.shape, 1) < HALF
+        ref[pl.ds(first, rows, stride=2), :] = value
+        ref[pl.ds(first + 1, rows, stride=2), :] = jnp.where(first_half, turned, after)
+
     def spread_current(c, value):
-        ext[pl.ds(c * ext_rows, own_rows, stride=2), :] = value
-        ext[pl.ds(c * ext_rows + 1, own_rows, stride=2), :] = value
+        spread_halves(ext, c * ext_rows, value)
         ext[pl.ds(c * ext_rows + 2 * own_rows, 8), :] = ext[pl.ds(c * ext_rows, 8), :]
 
     finish(flying)
@@ -216,7 +235,7 @@
             for r in range(cell_rows):
                 got = take_lanes(spread_row(slope_s, c * cell_rows + r), cell_lane)
                 slope = jnp.where(cell_at == r, got, slope)
-            v = vel_s[pl.ds(k * 64 + c, 8, stride=8), :]
+            v = vel_s[pl.ds(k * 24 + c, 8, stride=3), :]
             free_s[pl.ds(pl.multiple_of(c * own_rows + k * 8, 8), 8), :] = (
                 v - TIME_STEP * (drag + mass) * slope
             ) / (1.0 + TIME_STEP * drag)
@@ -225,42 +244,45 @@
     lax.fori_loop(0, own_rows // 8, free, 0, unroll=2)
     for c in range(3):
         spread_current(c, free_s[c * own_rows : (c + 1) * own_rows, :])
-    pick_bound()
-    flying = exchange(1, lambda g: ghost_out, lambda g: ghost_in.at[0, g])
+    pick_bound(0)
+    flying = exchange(1, lambda g: ghost_out.at[0], lambda g: ghost_in.at[0, g])
 
     iotas = [
         (lax.broadcasted_iota(jnp.int32, (16, LANES), 0) + 16 * q).astype(F32).astype(BF16)
-        for q in range(8)
+        for q in range(HALF // 16)
     ]
-    one, zero16 = jnp.ones((16, LANES), BF16), jnp.zeros((16, LANES), BF16)
+    signs = [jnp.full((16, LANES), sign, BF16) for sign in (1.0, -1.0)]
+    zero16 = jnp.zeros((16, LANES), BF16)
 
     def build(t, carry):
         for e in range(2):
-            row = lanes_s[pl.ds(e * tiles + t, 1), :].astype(F32)
-            row = jnp.broadcast_to(row, (16, LANES)).astype(BF16)
-            for q in range(8):
-                table[
-                    pl.ds(pl.multiple_of(t * LANES + 16 * q, 16), 16), e * LANES : (e + 1) * LANES
-                ] = jnp.where(iotas[q] == row, one, zero16)
+            row = jnp.broadcast_to(spots[pl.ds(e * tiles + t, 1), :], (16, LANES)).astype(BF16)
+            for q in range(HALF // 16):
+                at = slice(e * HALF + 16 * q, e * HALF + 16 * (q + 1))
+                table[t, at, :] = jnp.where(iotas[q] == row, signs[e], zero16)
         return carry
 
-    lax.fori_loop(0, tiles, build, 0, unroll=2)
-    for i in range(16):
-        left[i * ROWS + 24 : (i + 1) * ROWS, :] = jnp.zeros((8, LANES), F32)
+    lax.fori_loop(0, tiles, build, 0, unroll=4)
+    for i in range(32):
+        left[i * PITCH + 36 : i * PITCH + ROWS, :] = jnp.zeros((12, LANES), F32)
 
     nt = (((1,), (1,)), ((), ()))
     for sweep in range(SWEEPS):
         finish(flying)
         for c in range(3):
-            for g in range(4):
-                ghost_s[c * gpad + g * side_rows : c * gpad + (g + 1) * side_rows, :] = ghost_in[
-                    sweep, g, c * side_rows : (c + 1) * side_rows, :
-                ]
-            ghost_s[c * gpad + ghost_rows : c * gpad + ghost_rows + 1, :] = ghost_in[
-                sweep, 0, c * side_rows : c * side_rows + 1, :
-            ]
-
-        def contacts(u, carry):
+            spread_halves(
+                ghost_s,
+                c * gpad,
+                jnp.concatenate(
+                    [
+                        ghost_in[sweep, g, c * side_rows : (c + 1) * side_rows, :]
+                        for g in range(4)
+                    ],
+                    axis=0,
+                ),
+            )
+
+        def contacts(u, odd):
             at = pl.ds(pl.multiple_of(u * 8, 8), 8)
             code, lanes = [], []
             for e in range(2):
@@ -269,14 +291,19 @@
                 lanes.append(lanes_s[end_at, :])
             relative = []
             for c in range(3):
-                own = [ext[pl.ds(c * ext_rows + u * 8 + 2 * h, 8), :] for h in range(3)]
-                own += [spread_row(ghost_s, c * gpad + u + h) for h in range(2)]
+                near = ext[pl.ds(c * ext_rows + u * 8, 8), :]
+                next_ = ext[pl.ds(c * ext_rows + u * 8 + 2, 8), :]
+                far = jnp.where(
+                    row_iota < 4,
+                    spread_row(ghost_s, c * gpad + 2 * u),
+                    spread_row(ghost_s, c * gpad + 2 * u + 1),
+                )
                 ends_val = []
                 for e in range(2):
-                    val = take_lanes(own[4], lanes[e])
-                    for h in range(3, -1, -1):
-                        val = jnp.where(code[e] == h, take_lanes(own[h], lanes[e]), val)
-                    ends_val.append(val)
+                    val = jnp.where(
+                        code[e] < 4, take_lanes(next_, lanes[e]), take_lanes(far, lanes[e])
+                    )
+                    ends_val.append(jnp.where(code[e] < 2, take_lanes(near, lanes[e]), val))
                 relative.append(ends_val[0] - ends_val[1])
             part = lambda k: stage[pl.ds(u * (8 * STAGE) + k, 8, stride=STAGE), :]
             fr = [part(k) for k in range(9)]
@@ -289,7 +316,7 @@
             ]
             trial = []
             for k in range(3):
-                before = part(32 + k) if sweep == 0 else out_imp[k, at, :]
+                before = part(32 + k)
                 trial.append(
                     before
                     - (
@@ -304,65 +331,99 @@
             factor = jnp.minimum(1.0, FRICTION * normal / jnp.maximum(tangent, FLOOR_VALUE))
             imp = [normal * active, factor * trial[1] * active, factor * trial[2] * active]
             for k in range(3):
-                out_imp[k, at, :] = imp[k]
+                stage[pl.ds(u * (8 * STAGE) + 32 + k, 8, stride=STAGE), :] = imp[k]
             for c in range(3):
                 push = fr[c] * imp[0] + fr[3 + c] * imp[1] + fr[6 + c] * imp[2]
                 high = push.astype(BF16).astype(F32)
                 for s, term in enumerate((high, push - high)):
                     for e in range(2):
-                        signed = term if e == 0 else -term
-                        for h in range(5):
+                        for h in range(6):
                             left[
-                                pl.ds(e * 8 * ROWS + (h * 3 + c) * 2 + s, 8, stride=ROWS), :
-                            ] = jnp.where(code[e] == h, signed, 0.0)
-            for q in range(4):
+                                pl.ds((e * 8 + odd) * PITCH + (h * 3 + c) * 2 + s, 8, stride=PITCH), :
+                            ] = jnp.where(code[e] == h, term, 0.0)
+            ghost_sum = None
+            for i in range(8):
+                got = lax.dot_general(
+                    jnp.concatenate(
+                        [
+                            left[(odd + i) * PITCH : (odd + i) * PITCH + ROWS, :].astype(BF16),
+                            left[(odd + i + 8) * PITCH : (odd + i + 8) * PITCH + ROWS, :].astype(BF16),
+                        ],
+                        axis=1,
+                    ),
+                    jnp.concatenate(
+                        [
+                            table[u * 8 + i, e * HALF : (e + 1) * HALF, :]
+                            for e in range(2)
+                        ],
+                        axis=1,
+                    ),
+                    nt,
+                    preferred_element_type=F32,
+                )
+                at = ((i & 1) * own_part + u * 4 + (i >> 1) + 2) * OWN_PITCH
+                sums[pl.ds(at, 24), 0:HALF] = got[0:24]
+                ghost_sum = got[24:40] if i % 4 == 0 else ghost_sum + got[24:40]
+                if i % 4 == 3:
+                    at = ((i >> 2) * ghost_part + u + 1) * GHOST_PITCH
+                    ghost_sums[pl.ds(at, 16), 0:HALF] = ghost_sum
+
+        def two(k, carry):
+            contacts(2 * k, 0)
+            contacts(2 * k + 1, 16)
+            return carry
+
+        lax.fori_loop(0, tiles // 16, two, 0, unroll=2)
+        for par in range(2):
+            base = par * ghost_part * GHOST_PITCH
+            ghost_sums[base : base + GHOST_PITCH, :] = ghost_sums[
+                base + ghost_rows * GHOST_PITCH : base + (ghost_rows + 1) * GHOST_PITCH, :
+            ]
+            base = par * own_part * OWN_PITCH
+            sums[base : base + 2 * OWN_PITCH, :] = sums[
+                base + own_rows * OWN_PITCH : base + (own_rows + 2) * OWN_PITCH, :
+            ]
+        first_half = lax.broadcasted_iota(jnp.int32, (8, LANES), 1) < HALF
+
+        def gather_halves(ref, part_rows, pitch, pad, r, terms):
+            halves = []
+            for par in range(2):
                 total = None
-                for i in (2 * q, 2 * q + 1):
-                    got = lax.dot_general(
-                        jnp.concatenate(
-                            [
-                                left[i * ROWS : (i + 1) * ROWS, :].astype(BF16),
-                                left[(i + 8) * ROWS : (i + 9) * ROWS, :].astype(BF16),
-                            ],
-                            axis=1,
-                        ),
-                        table[pl.ds(pl.multiple_of((u * 8 + i) * LANES, LANES), LANES), :],
-                        nt,
-                        preferred_element_type=F32,
-                    )
-                    total = got if total is None else total + got
-                sums[pl.ds(pl.multiple_of((u * 4 + q + 4) * ROWS, ROWS), ROWS), :] = total
-            return carry
-
-        lax.fori_loop(0, tiles // 8, contacts, 0, unroll=8)
-        sums[0 : 4 * ROWS, :] = sums[pairs * ROWS : (pairs + 4) * ROWS, :]
+                for h, row in terms:
+                    for s in range(2):
+                        block = par - h
+                        first = ((block & 1) * part_rows + r + (block >> 1) + pad) * pitch + row + s
+                        got = ref[pl.ds(first, 8, stride=pitch), :]
+                        total = got if total is None else total + got
+                halves.append(total)
+            return jnp.where(first_half, halves[0], pltpu.roll(halves[1], HALF, 1))
 
         for c in range(3):
             for r in range(0, ghost_rows, 8):
-                total = None
-                for h in range(2):
-                    for q in range(4):
-                        for s in range(2):
-                            first = (4 * (r - h) + q + 4) * ROWS + ((3 + h) * 3 + c) * 2 + s
-                            got = sums[pl.ds(first, 8, stride=4 * ROWS), :]
-                            total = got if total is None else total + got
+                terms = [(h, h * 6 + c * 2) for h in range(2)]
+                total = gather_halves(ghost_sums, ghost_part, GHOST_PITCH, 1, r, terms)
                 for i in range(0, 8, side_rows):
                     sum_out[
-                        (r + i) // side_rows, c * side_rows : (c + 1) * side_rows, :
+                        sweep, (r + i) // side_rows, c * side_rows : (c + 1) * side_rows, :
                     ] = total[i : i + side_rows]
-        flying = exchange(2 + 2 * sweep, lambda g: sum_out.at[g], lambda g: sum_in.at[sweep, g])
+        flying = exchange(2 + 2 * sweep, lambda g: sum_out.at[sweep, g], lambda g: sum_in.at[sweep, g])
         own_total = []
         for c in range(3):
             parts = []
             for r in range(0, own_rows, 8):
-                total = None
-                for h in range(3):
-                    for s in range(2):
-                        first = (r - h + 4) * ROWS + (h * 3 + c) * 2 + s
-                        got = sums[pl.ds(first, 8, stride=ROWS), :]
-                        total = got if total is None else total + got
-                parts.append(total)
+                terms = [(h, h * 6 + c * 2) for h in range(4)]
+                parts.append(gather_halves(sums, own_part, OWN_PITCH, 2, r, terms))
             own_total.append(jnp.concatenate(parts, axis=0))
+        if sweep == SWEEPS - 1:
+
+            def unstage(t, carry):
+                cols = pl.ds(pl.multiple_of(t * LANES, LANES), LANES)
+                start_ref[:, cols] = stage[pl.ds(t * STAGE + 32, 3), :]
+                return carry
+
+            lax.fori_loop(0, tiles, unstage, 0, unroll=8)
+            imp_store = pltpu.make_async_copy(start_ref, out_imp, load_sem.at[0])
+            imp_store.start()
         finish(flying)
         received = (
             sum_in[sweep, 0] + sum_in[sweep, 1] + sum_in[sweep, 2] + sum_in[sweep, 3]
@@ -390,12 +451,25 @@
             if sweep < SWEEPS - 1:
                 spread_current(c, current)
             else:
-                out_vel[c] = current
+                vel_s[pl.ds(c, own_rows, stride=3), :] = current
         if sweep < SWEEPS - 1:
-            pick_bound()
+            pick_bound(sweep + 1)
             flying = exchange(
-                3 + 2 * sweep, lambda g: ghost_out, lambda g: ghost_in.at[sweep + 1, g]
+                3 + 2 * sweep, lambda g: ghost_out.at[sweep + 1], lambda g: ghost_in.at[sweep + 1, g]
             )
+
+    def unstage_grain(t, carry):
+        cols = pl.ds(pl.multiple_of(t * LANES, LANES), LANES)
+        vel_ref[:, cols] = vel_s[pl.ds(t * 3, 3), :]
+        return carry
+
+    lax.fori_loop(0, own_rows, unstage_grain, 0, unroll=8)
+    vel_store = pltpu.make_async_copy(vel_ref, out_vel, load_sem.at[1])
+    vel_store.start()
+    for copy in sent:
+        copy.wait_send()
+    imp_store.wait()
+    vel_store.wait()
 
 
 def solution(mesh):
@@ -409,17 +483,16 @@
         tiles = contact_pair.shape[1] // LANES
         side_rows = boundary_list.shape[0] // LANES
         cell_rows = pressure.size // LANES
-        gpad = 4 * side_rows + 8
+        gpad = 8 * side_rows
         rounds = 1 + 2 * SWEEPS
-        vmem = pl.BlockSpec(memory_space=pltpu.VMEM)
         out_vel, out_imp = pl.pallas_call(
             lambda *refs: step_kernel(sizes, *refs),
             out_shape=(
-                jax.ShapeDtypeStruct((3, own_rows, LANES), F32),
-                jax.ShapeDtypeStruct((3, tiles, LANES), F32),
+                jax.ShapeDtypeStruct(velocity.shape, F32),
+                jax.ShapeDtypeStruct(impulse_start.shape, F32),
             ),
             in_specs=[pl.BlockSpec(memory_space=pltpu.HBM)] * 12,
-            out_specs=(vmem, vmem),
+            out_specs=(pl.BlockSpec(memory_space=pltpu.HBM),) * 2,
             scratch_shapes=[
                 pltpu.VMEM((3, velocity.shape[1]), F32),
                 pltpu.VMEM((own_rows, LANES), F32),
@@ -438,20 +511,22 @@
                 pltpu.VMEM((4, cell_rows, LANES), F32),
                 pltpu.VMEM((SWEEPS, 4, 3 * side_rows, LANES), F32),
                 pltpu.VMEM((SWEEPS, 4, 3 * side_rows, LANES), F32),
-                pltpu.VMEM((3 * side_rows, LANES), F32),
-                pltpu.VMEM((4, 3 * side_rows, LANES), F32),
+                pltpu.VMEM((SWEEPS, 3 * side_rows, LANES), F32),
+                pltpu.VMEM((SWEEPS, 4, 3 * side_rows, LANES), F32),
                 pltpu.VMEM((3 * cell_rows, LANES), F32),
-                pltpu.VMEM((own_rows * 8, LANES), F32),
+                pltpu.VMEM((own_rows * 3, LANES), F32),
                 pltpu.VMEM((3 * own_rows, LANES), F32),
                 pltpu.VMEM((tiles * STAGE, LANES), F32),
-                pltpu.VMEM((tiles * 8, LANES), jnp.int32),
+                pltpu.VMEM((tiles * 3, LANES), jnp.int32),
                 pltpu.VMEM((2 * tiles, LANES), jnp.int32),
                 pltpu.VMEM((2 * tiles, LANES), jnp.int32),
-                pltpu.VMEM((tiles * LANES, 2 * LANES), BF16),
+                pltpu.VMEM((2 * tiles, LANES), F32),
+                pltpu.VMEM((tiles, LANES, LANES), BF16),
                 pltpu.VMEM((3 * (2 * own_rows + 8), LANES), F32),
                 pltpu.VMEM((3 * gpad, LANES), F32),
-                pltpu.VMEM((16 * ROWS, LANES), F32),
-                pltpu.VMEM(((tiles // 2 + 4) * ROWS, LANES), F32),
+                pltpu.VMEM((32 * PITCH, LANES), F32),
+                pltpu.VMEM((2 * (own_rows + 2) * OWN_PITCH, LANES), F32),
+                pltpu.VMEM((2 * (4 * side_rows + 1) * GHOST_PITCH, LANES), F32),
                 pltpu.VMEM((LANES, side_rows * LANES), BF16),
                 pltpu.VMEM((own_rows, side_rows * LANES), BF16),
                 pltpu.SemaphoreType.DMA((rounds, 4)),
@@ -475,7 +550,7 @@
             contact_mask.reshape(tiles, LANES),
             pressure,
         )
-        return out_vel.reshape(3, -1), out_imp.reshape(3, -1)
+        return out_vel, out_imp
 
     grains, lists = P(("gx", "gy")), P(None, ("gx", "gy"))
     return jax.shard_map(

time: 40.7 us -> 34.5 us (0.85)
  Pallas kernels: 37.4 us -> 31.3 us
    pallas_call x1, Pallas kernels: 37.4 us -> 31.3 us  [local(): pl.pallas_call(lambda *refs: step_kernel(sizes, *refs), out_shape=(jax.Sh...]
where the time goes in v1:
time: 34.5 us; the launch traced here: 34.3 us
  Pallas kernels  31.3 us (91%)
  local copies, waits for them, and re-layouts  2.33 us (7%)
  between operations  0.65 us (2%)
    pallas_call x1, Pallas kernels, local(): pl.pallas_call(lambda *refs: step_kernel(sizes, *refs), out_shape=(jax.Sh...  31.3 us
    unnamed x4, local copies, waits for them, and re-layouts  2.33 us

profile of v1, /device:TPU:0, one launch (start us, length us, event | category | flops | bytes accessed | tf_op | source)
XLA Modules:
  0.0 34.3 jit_solution(12521003982234545349)
XLA Ops:
  0.6 31.3 %shard_map.131 = (f32[3,8192]{1,0:T(4,128)}, f32[3,16384]{1,0:T(4,128)}) custom-call(f32[3,8192]{1,0:T(4,128)} %refs_0_.1, f32[64,128]{1,0:T(8,128)} %bitcast.6, f32[64,128]{1,0:T(8,128)} %bitcast.7, s32[64,128]{1,0:T(8,128)} %bitcast.8, s32[4,128]{1,0:T(4,128)} %bitcast.9, s32[2,16384]{1,0:T(2,128)} %refs_5_.1, f32[9,16384]{1,0:T(8,128)} %refs_6_.1, ...), custom_call_target="tpu_custom_call" | custom-call | tf_op jit(solution)/shard_map/pallas_call | solution.py:488
  32.0 0.0 copy-start
  32.0 1.6 %copy.16 = f32[3,8192]{1,0:T(4,128)} copy(f32[3,8192]{1,0:T(4,128)} %get-tuple-element.4) | data formatting | bytes 196608
  33.6 0.0 copy-done
  33.6 0.7 %copy.17 = f32[3,16384]{1,0:T(4,128)} copy(f32[3,16384]{1,0:T(4,128)S(1)} %copy-done) | data formatting | bytes 393216
Async XLA Ops:
  32.0 1.6 %copy-start = (f32[3,16384]{1,0:T(4,128)S(1)}, f32[3,16384]{1,0:T(4,128)}, u32[]{:S(2)}) copy-start(f32[3,16384]{1,0:T(4,128)} %get-tuple-element.5) | copy-start | bytes 589828

commit v2 on v1

--- a/solution.py
+++ b/solution.py
@@ -18,6 +18,9 @@
 GHOST_PITCH = 17
 F32 = jnp.float32
 BF16 = jnp.bfloat16
+NEAR = ((-1, 0), (1, 0), (0, -1), (0, 1))
+FAR = ((-2, 0), (2, 0), (0, -2), (0, 2), (-1, -1), (-1, 1), (1, -1), (1, 1))
+AROUND = NEAR + FAR
 
 
 def take_lanes(values, lanes):
@@ -35,10 +38,10 @@
     out_vel, out_imp,
     vel_ref, mass_ref, drag_ref, cell_ref, bound_ref, pair_ref, frame_ref, block_ref,
     start_ref, gap_ref, mask_ref, pres_raw, pres_wide, pres_ref,
-    pres_in, ghost_in, sum_in, ghost_out, sum_out,
-    slope_s, vel_s, free_s, stage, ends, codes, lanes_s, spots, table, ext, ghost_s,
+    pres_in, grain_in, grain_out, ghost_in, sum_in, ghost_out, sum_out,
+    slope_s, slope_n, vel_s, free_s, stage, ends, codes, lanes_s, spots, table, ext, ghost_s,
     left, sums, ghost_sums, bound_hot, bound_row,
-    send_sem, recv_sem, load_sem,
+    send_sem, recv_sem, pres_send, pres_recv, load_sem,
 ):
     nx, ny = sizes
     tiles = mask_ref.shape[0]
@@ -55,21 +58,18 @@
     row_iota = lax.broadcasted_iota(jnp.int32, (8, LANES), 0)
 
     mx, my = lax.axis_index("gx"), lax.axis_index("gy")
-    sides = (
-        (lax.rem(mx + nx - 1, nx), my),
-        (lax.rem(mx + 1, nx), my),
-        (mx, lax.rem(my + ny - 1, ny)),
-        (mx, lax.rem(my + 1, ny)),
-    )
+    reach = lambda dx, dy: (lax.rem(mx + dx + 2 * nx, nx), lax.rem(my + dy + 2 * ny, ny))
+    sides = [reach(dx, dy) for dx, dy in NEAR]
+    others = [k for k, (dx, dy) in enumerate(AROUND) if dx % nx or dy % ny]
 
     loads = [
         pltpu.make_async_copy(source, target, load_sem.at[k])
         for k, (source, target) in enumerate(
             (
-                (pair_hbm, pair_ref), (frame_hbm, frame_ref), (block_hbm, block_ref),
-                (start_hbm, start_ref), (gap_hbm, gap_ref), (vel_hbm, vel_ref),
-                (bound_hbm, bound_ref), (cell_hbm, cell_ref), (drag_hbm, drag_ref),
-                (mass_hbm, mass_ref), (mask_hbm, mask_ref),
+                (vel_hbm, vel_ref), (bound_hbm, bound_ref), (drag_hbm, drag_ref),
+                (mass_hbm, mass_ref), (cell_hbm, cell_ref), (pair_hbm, pair_ref),
+                (mask_hbm, mask_ref), (start_hbm, start_ref), (gap_hbm, gap_ref),
+                (frame_hbm, frame_ref), (block_hbm, block_ref),
             )
         )
     ]
@@ -79,8 +79,10 @@
         load.start()
 
     barrier = pltpu.get_barrier_semaphore()
-    for side in sides:
-        pl.semaphore_signal(barrier, inc=1, device_id=side, device_id_type=pl.DeviceIdType.MESH)
+    for k in others:
+        pl.semaphore_signal(
+            barrier, inc=1, device_id=reach(*AROUND[k]), device_id_type=pl.DeviceIdType.MESH
+        )
 
     lane = lax.broadcasted_iota(jnp.int32, (cell_rows, LANES), 1)
     pres_load.wait()
@@ -92,8 +94,6 @@
         piece = pltpu.roll(pres_wide[pl.ds(k, cell_rows, stride=per_row), :], k * width, 1)
         p = jnp.where(lane < k * width, p, piece)
     pres_ref[...] = p
-    pl.semaphore_wait(barrier, 4)
-
     def exchange(step, source, target):
         copies = []
         for g in range(4):
@@ -118,9 +118,63 @@
             copy.wait_recv()
         sent.extend(copies)
 
-    flying = exchange(0, lambda g: pres_ref, lambda g: pres_in.at[g])
-
-    for load in loads:
+    for load in loads[:5]:
+        load.wait()
+    bound_all = bound_ref[...]
+    bound_lane = bound_all & (LANES - 1)
+    bound_at = bound_all >> 7
+    two_lane = jnp.concatenate([bound_lane, bound_lane], axis=0)
+    two_at = jnp.concatenate([bound_at, bound_at], axis=0)
+    half = own_rows // 2
+    upper = row_iota < side_rows
+    low_at = two_at < half
+
+    def pick(row_of, kinds):
+        def body(k, acc):
+            acc = list(acc)
+            for i in range(4):
+                r = k * 4 + i
+                hit = two_at == jnp.where(upper, r, r + half)
+                for c in range(len(kinds)):
+                    got = take_lanes(jnp.where(upper, row_of(c, r), row_of(c, r + half)), two_lane)
+                    acc[c] = jnp.where(hit, got, acc[c])
+            return tuple(acc)
+
+        start = tuple(jnp.zeros((8, LANES), kind) for kind in kinds)
+        acc = lax.fori_loop(0, half // 4, body, start, unroll=2)
+        return [
+            jnp.where(low_at[:side_rows], got[:side_rows], got[side_rows:]) for got in acc
+        ]
+
+    def grain_row(c, r):
+        if c < 3:
+            cols = pl.ds(pl.multiple_of(r * LANES, LANES), LANES)
+            return jnp.broadcast_to(vel_ref[pl.ds(c, 1), cols], (8, LANES))
+        return spread_row((drag_ref, mass_ref, cell_ref)[c - 3], r)
+
+    *moving, drag_b, mass_b, cell_b = pick(grain_row, (F32,) * 5 + (jnp.int32,))
+    below = 1.0 + TIME_STEP * drag_b
+    for c in range(3):
+        grain_out[c * side_rows : (c + 1) * side_rows, :] = moving[c] / below
+    grain_out[3 * side_rows : 4 * side_rows, :] = TIME_STEP * (drag_b + mass_b) / below
+    grain_out[4 * side_rows : 5 * side_rows, :] = cell_b.astype(F32)
+    pl.semaphore_wait(barrier, len(others))
+    spreading = {}
+    for k in others:
+        dx, dy = AROUND[k]
+        back = AROUND.index((-dx, -dy))
+        spreading[back] = pltpu.make_async_remote_copy(
+            src_ref=pres_ref,
+            dst_ref=pres_in.at[back],
+            send_sem=pres_send.at[k],
+            recv_sem=pres_recv.at[back],
+            device_id=reach(dx, dy),
+            device_id_type=pl.DeviceIdType.MESH,
+        )
+    for copy in spreading.values():
+        copy.start()
+    flying = exchange(0, lambda g: grain_out, lambda g: grain_in.at[g])
+    for load in loads[5:]:
         load.wait()
 
     def stage_tile(t, carry):
@@ -158,41 +212,17 @@
 
     lax.fori_loop(0, tiles // 8, place, 0, unroll=2)
 
-    bound_all = bound_ref[...]
-    bound_lane = bound_all & (LANES - 1)
-    bound_at = bound_all >> 7
     hot_iota = lax.broadcasted_iota(jnp.int32, (LANES, LANES), 0)
     row_hot = lax.broadcasted_iota(jnp.int32, (own_rows, LANES), 0)
     for q in range(side_rows):
         cols = slice(q * LANES, (q + 1) * LANES)
         bound_hot[:, cols] = jnp.where(hot_iota == bound_lane[q : q + 1], 1.0, 0.0).astype(BF16)
         bound_row[:, cols] = jnp.where(row_hot == bound_at[q : q + 1], 1.0, 0.0).astype(BF16)
-    two_lane = jnp.concatenate([bound_lane, bound_lane], axis=0)
-    two_at = jnp.concatenate([bound_at, bound_at], axis=0)
-    half = own_rows // 2
-    upper = row_iota < side_rows
 
     def pick_bound(turn):
-        def body(k, acc):
-            acc = list(acc)
-            for i in range(4):
-                r = k * 4 + i
-                hit = two_at == jnp.where(upper, r, r + half)
-                for c in range(3):
-                    low = spread_row(ext, c * ext_rows + 2 * r)
-                    high = spread_row(ext, c * ext_rows + 2 * (r + half))
-                    got = take_lanes(jnp.where(upper, low, high), two_lane)
-                    acc[c] = jnp.where(hit, got, acc[c])
-            return tuple(acc)
-
-        zero = jnp.zeros((8, LANES), F32)
-        acc = lax.fori_loop(0, half // 4, body, (zero, zero, zero), unroll=4)
-        low_at = two_at < half
+        got = pick(lambda c, r: spread_row(ext, c * ext_rows + 2 * r), (F32,) * 3)
         for c in range(3):
-            got = acc[c]
-            ghost_out[turn, c * side_rows : (c + 1) * side_rows, :] = jnp.where(
-                low_at[:side_rows], got[:side_rows], got[side_rows:]
-            )
+            ghost_out[turn, c * side_rows : (c + 1) * side_rows, :] = got[c]
 
     def spread_halves(ref, first, value):
         rows = value.shape[0]
@@ -206,24 +236,55 @@
         spread_halves(ext, c * ext_rows, value)
         ext[pl.ds(c * ext_rows + 2 * own_rows, 8), :] = ext[pl.ds(c * ext_rows, 8), :]
 
-    finish(flying)
-
+    iotas = [
+        (lax.broadcasted_iota(jnp.int32, (16, LANES), 0) + 16 * q).astype(F32).astype(BF16)
+        for q in range(HALF // 16)
+    ]
+    signs = [jnp.full((16, LANES), sign, BF16) for sign in (1.0, -1.0)]
+    zero16 = jnp.zeros((16, LANES), BF16)
+
+    def build(t, carry):
+        for e in range(2):
+            row = jnp.broadcast_to(spots[pl.ds(e * tiles + t, 1), :], (16, LANES)).astype(BF16)
+            for q in range(HALF // 16):
+                at = slice(e * HALF + 16 * q, e * HALF + 16 * (q + 1))
+                table[t, at, :] = jnp.where(iotas[q] == row, signs[e], zero16)
+        return carry
+
+    lax.fori_loop(0, tiles, build, 0, unroll=4)
+    for i in range(32):
+        left[i * PITCH + 36 : i * PITCH + ROWS, :] = jnp.zeros((12, LANES), F32)
+
+    for k in range(4):
+        spreading[k].wait_recv()
     even = (lax.broadcasted_iota(jnp.int32, (cell_rows, LANES), 0) & 1) == 0
     up1 = lambda a: jnp.concatenate([a[1:], a[:1]], axis=0)
     down1 = lambda a: jnp.concatenate([a[-1:], a[:-1]], axis=0)
     turn = lambda a, n: pltpu.roll(a, n % LANES, 1)
-    p_next = turn(p, -16)
-    plus = jnp.where(lane < 112, p_next, jnp.where(even, up1(p_next), down1(turn(pres_in[1], -16))))
-    p_prev = turn(p, 16)
-    minus = jnp.where(lane >= 16, p_prev, jnp.where(even, up1(turn(pres_in[0], 16)), down1(p_prev)))
-    slope_s[0:cell_rows] = (plus - minus) * 0.5
-    plus = jnp.where((lane & 15) < 15, turn(p, -1), turn(pres_in[3], 15))
-    minus = jnp.where((lane & 15) > 0, turn(p, 1), turn(pres_in[2], -15))
-    slope_s[cell_rows : 2 * cell_rows] = (plus - minus) * 0.5
     none = jnp.zeros((2, LANES), F32)
-    slope_s[2 * cell_rows : 3 * cell_rows] = (
-        jnp.concatenate([p[2:], none], axis=0) - jnp.concatenate([none, p[:-2]], axis=0)
-    ) * 0.5
+
+    def pres_at(dx, dy):
+        if dx % nx == 0 and dy % ny == 0:
+            return p
+        return pres_in[AROUND.index((dx, dy))]
+
+    def slopes(ref, first, dx, dy):
+        mid = pres_at(dx, dy)
+        prev_x, next_x = pres_at(dx - 1, dy), pres_at(dx + 1, dy)
+        prev_y, next_y = pres_at(dx, dy - 1), pres_at(dx, dy + 1)
+        after = turn(mid, -16)
+        plus = jnp.where(lane < 112, after, jnp.where(even, up1(after), down1(turn(next_x, -16))))
+        before = turn(mid, 16)
+        minus = jnp.where(lane >= 16, before, jnp.where(even, up1(turn(prev_x, 16)), down1(before)))
+        ref[first : first + cell_rows] = (plus - minus) * 0.5
+        plus = jnp.where((lane & 15) < 15, turn(mid, -1), turn(next_y, 15))
+        minus = jnp.where((lane & 15) > 0, turn(mid, 1), turn(prev_y, -15))
+        ref[first + cell_rows : first + 2 * cell_rows] = (plus - minus) * 0.5
+        ref[first + 2 * cell_rows : first + 3 * cell_rows] = (
+            jnp.concatenate([mid[2:], none], axis=0) - jnp.concatenate([none, mid[:-2]], axis=0)
+        ) * 0.5
+
+    slopes(slope_s, 0, 0, 0)
 
     def free(k, carry):
         at = pl.ds(pl.multiple_of(k * 8, 8), 8)
@@ -244,44 +305,38 @@
     lax.fori_loop(0, own_rows // 8, free, 0, unroll=2)
     for c in range(3):
         spread_current(c, free_s[c * own_rows : (c + 1) * own_rows, :])
-    pick_bound(0)
-    flying = exchange(1, lambda g: ghost_out.at[0], lambda g: ghost_in.at[0, g])
-
-    iotas = [
-        (lax.broadcasted_iota(jnp.int32, (16, LANES), 0) + 16 * q).astype(F32).astype(BF16)
-        for q in range(HALF // 16)
-    ]
-    signs = [jnp.full((16, LANES), sign, BF16) for sign in (1.0, -1.0)]
-    zero16 = jnp.zeros((16, LANES), BF16)
-
-    def build(t, carry):
-        for e in range(2):
-            row = jnp.broadcast_to(spots[pl.ds(e * tiles + t, 1), :], (16, LANES)).astype(BF16)
-            for q in range(HALF // 16):
-                at = slice(e * HALF + 16 * q, e * HALF + 16 * (q + 1))
-                table[t, at, :] = jnp.where(iotas[q] == row, signs[e], zero16)
-        return carry
-
-    lax.fori_loop(0, tiles, build, 0, unroll=4)
-    for i in range(32):
-        left[i * PITCH + 36 : i * PITCH + ROWS, :] = jnp.zeros((12, LANES), F32)
+    for k in others[4:]:
+        spreading[k].wait_recv()
+    sent.extend(spreading.values())
+    finish(flying)
+    for g in range(4):
+        slopes(slope_n, 3 * cell_rows * g, *NEAR[g])
+    ghost_free = [[], [], []]
+    for g in (0, 2):
+        both = [
+            jnp.concatenate(
+                [grain_in[g + i, k * side_rows : (k + 1) * side_rows, :] for i in range(2)], axis=0
+            )
+            for k in range(5)
+        ]
+        cells = both[4].astype(jnp.int32)
+        cell_at, cell_lane = cells >> 7, cells & (LANES - 1)
+        for c in range(3):
+            slope = jnp.zeros((8, LANES), F32)
+            for r in range(cell_rows):
+                first = (3 * g + c) * cell_rows + r
+                row = jnp.where(
+                    row_iota < side_rows,
+                    spread_row(slope_n, first),
+                    spread_row(slope_n, first + 3 * cell_rows),
+                )
+                slope = jnp.where(cell_at == r, take_lanes(row, cell_lane), slope)
+            ghost_free[c].append(both[c] - both[3] * slope)
+    for c in range(3):
+        spread_halves(ghost_s, c * gpad, jnp.concatenate(ghost_free[c], axis=0))
 
     nt = (((1,), (1,)), ((), ()))
     for sweep in range(SWEEPS):
-        finish(flying)
-        for c in range(3):
-            spread_halves(
-                ghost_s,
-                c * gpad,
-                jnp.concatenate(
-                    [
-                        ghost_in[sweep, g, c * side_rows : (c + 1) * side_rows, :]
-                        for g in range(4)
-                    ],
-                    axis=0,
-                ),
-            )
-
         def contacts(u, odd):
             at = pl.ds(pl.multiple_of(u * 8, 8), 8)
             code, lanes = [], []
@@ -406,7 +461,7 @@
                     sum_out[
                         sweep, (r + i) // side_rows, c * side_rows : (c + 1) * side_rows, :
                     ] = total[i : i + side_rows]
-        flying = exchange(2 + 2 * sweep, lambda g: sum_out.at[sweep, g], lambda g: sum_in.at[sweep, g])
+        flying = exchange(1 + 2 * sweep, lambda g: sum_out.at[sweep, g], lambda g: sum_in.at[sweep, g])
         own_total = []
         for c in range(3):
             parts = []
@@ -453,10 +508,23 @@
             else:
                 vel_s[pl.ds(c, own_rows, stride=3), :] = current
         if sweep < SWEEPS - 1:
-            pick_bound(sweep + 1)
+            pick_bound(sweep)
             flying = exchange(
-                3 + 2 * sweep, lambda g: ghost_out.at[sweep + 1], lambda g: ghost_in.at[sweep + 1, g]
+                2 + 2 * sweep, lambda g: ghost_out.at[sweep], lambda g: ghost_in.at[sweep, g]
             )
+            finish(flying)
+            for c in range(3):
+                spread_halves(
+                    ghost_s,
+                    c * gpad,
+                    jnp.concatenate(
+                        [
+                            ghost_in[sweep, g, c * side_rows : (c + 1) * side_rows, :]
+                            for g in range(4)
+                        ],
+                        axis=0,
+                    ),
+                )
 
     def unstage_grain(t, carry):
         cols = pl.ds(pl.multiple_of(t * LANES, LANES), LANES)
@@ -470,6 +538,19 @@
         copy.wait_send()
     imp_store.wait()
     vel_store.wait()
+
+
+def hand_on(vel_in, imp_in, vel_out, imp_out, vel_ref, imp_ref, sem):
+    pairs = ((imp_in, imp_ref, imp_out), (vel_in, vel_ref, vel_out))
+    loads = [pltpu.make_async_copy(x, y, sem.at[0, k]) for k, (x, y, _) in enumerate(pairs)]
+    stores = [pltpu.make_async_copy(y, z, sem.at[1, k]) for k, (_, y, z) in enumerate(pairs)]
+    for load in loads:
+        load.start()
+    for load, store in zip(loads, stores):
+        load.wait()
+        store.start()
+    for store in stores:
+        store.wait()
 
 
 def solution(mesh):
@@ -484,7 +565,7 @@
         side_rows = boundary_list.shape[0] // LANES
         cell_rows = pressure.size // LANES
         gpad = 8 * side_rows
-        rounds = 1 + 2 * SWEEPS
+        rounds = 2 * SWEEPS
         out_vel, out_imp = pl.pallas_call(
             lambda *refs: step_kernel(sizes, *refs),
             out_shape=(
@@ -508,12 +589,15 @@
                 pltpu.VMEM(pressure.shape, F32),
                 pltpu.VMEM((pressure.size // pressure.shape[2], LANES), F32),
                 pltpu.VMEM((cell_rows, LANES), F32),
-                pltpu.VMEM((4, cell_rows, LANES), F32),
+                pltpu.VMEM((12, cell_rows, LANES), F32),
+                pltpu.VMEM((4, 5 * side_rows, LANES), F32),
+                pltpu.VMEM((5 * side_rows, LANES), F32),
+                pltpu.VMEM((SWEEPS - 1, 4, 3 * side_rows, LANES), F32),
                 pltpu.VMEM((SWEEPS, 4, 3 * side_rows, LANES), F32),
-                pltpu.VMEM((SWEEPS, 4, 3 * side_rows, LANES), F32),
-                pltpu.VMEM((SWEEPS, 3 * side_rows, LANES), F32),
+                pltpu.VMEM((SWEEPS - 1, 3 * side_rows, LANES), F32),
                 pltpu.VMEM((SWEEPS, 4, 3 * side_rows, LANES), F32),
                 pltpu.VMEM((3 * cell_rows, LANES), F32),
+                pltpu.VMEM((12 * cell_rows, LANES), F32),
                 pltpu.VMEM((own_rows * 3, LANES), F32),
                 pltpu.VMEM((3 * own_rows, LANES), F32),
                 pltpu.VMEM((tiles * STAGE, LANES), F32),
@@ -531,6 +615,8 @@
                 pltpu.VMEM((own_rows, side_rows * LANES), BF16),
                 pltpu.SemaphoreType.DMA((rounds, 4)),
                 pltpu.SemaphoreType.DMA((rounds, 4)),
+                pltpu.SemaphoreType.DMA((12,)),
+                pltpu.SemaphoreType.DMA((12,)),
                 pltpu.SemaphoreType.DMA((12,)),
             ],
             compiler_params=pltpu.CompilerParams(
@@ -550,7 +636,20 @@
             contact_mask.reshape(tiles, LANES),
             pressure,
         )
-        return out_vel, out_imp
+        return pl.pallas_call(
+            hand_on,
+            out_shape=(
+                jax.ShapeDtypeStruct(velocity.shape, F32),
+                jax.ShapeDtypeStruct(impulse_start.shape, F32),
+            ),
+            in_specs=[pl.BlockSpec(memory_space=pltpu.HBM)] * 2,
+            out_specs=(pl.BlockSpec(memory_space=pltpu.HBM),) * 2,
+            scratch_shapes=[
+                pltpu.VMEM(velocity.shape, F32),
+                pltpu.VMEM(impulse_start.shape, F32),
+                pltpu.SemaphoreType.DMA((2, 2)),
+            ],
+        )(out_vel, out_imp)
 
     grains, lists = P(("gx", "gy")), P(None, ("gx", "gy"))
     return jax.shard_map(

time: 34.5 us -> 32.2 us (0.933)
  local copies, waits for them, and re-layouts: 2.33 us -> 0 us
    unnamed x4 -> x0, local copies, waits for them, and re-layouts: 2.33 us -> none
    pallas_call x0 -> x1, Pallas kernels: none -> 1.73 us  [local(): pl.pallas_call(hand_on, out_shape=(jax.ShapeDtypeStruct(velocity.shape, F...]
    pallas_call x1, Pallas kernels: 31.3 us -> 29.7 us  [local(): pl.pallas_call(lambda *refs: step_kernel(sizes, *refs), out_shape=(jax.Sh...]
where the time goes in v2:
time: 32.2 us; the launch traced here: 32 us
  Pallas kernels  31.4 us (98%)
  between operations  0.64 us (2%)
    pallas_call x1, Pallas kernels, local(): pl.pallas_call(lambda *refs: step_kernel(sizes, *refs), out_shape=(jax.Sh...  29.7 us
    pallas_call x1, Pallas kernels, local(): pl.pallas_call(hand_on, out_shape=(jax.ShapeDtypeStruct(velocity.shape, F...  1.73 us

profile of v2, /device:TPU:0, one launch (start us, length us, event | category | flops | bytes accessed | tf_op | source)
XLA Modules:
  0.0 32.0 jit_solution(8914202041179310167)
XLA Ops:
  0.6 29.7 %shard_map.131 = (f32[3,8192]{1,0:T(4,128)}, f32[3,16384]{1,0:T(4,128)}) custom-call(f32[3,8192]{1,0:T(4,128)} %refs_0_.1, f32[64,128]{1,0:T(8,128)} %bitcast.6, f32[64,128]{1,0:T(8,128)} %bitcast.7, s32[64,128]{1,0:T(8,128)} %bitcast.8, s32[4,128]{1,0:T(4,128)} %bitcast.9, s32[2,16384]{1,0:T(2,128)} %refs_5_.1, f32[9,16384]{1,0:T(8,128)} %refs_6_.1, ...), custom_call_target="tpu_custom_call" | custom-call | tf_op jit(solution)/shard_map/pallas_call | solution.py:569
  30.3 1.7 %shard_map.132 = (f32[3,8192]{1,0:T(4,128)}, f32[3,16384]{1,0:T(4,128)}) custom-call(f32[3,8192]{1,0:T(4,128)} %get-tuple-element.4.vel_in, f32[3,16384]{1,0:T(4,128)} %get-tuple-element.5.imp_in), custom_call_target="tpu_custom_call" | custom-call | tf_op jit(solution)/shard_map/pallas_call | solution.py:639

commit v3 on v2

--- a/solution.py
+++ b/solution.py
@@ -21,6 +21,8 @@
 NEAR = ((-1, 0), (1, 0), (0, -1), (0, 1))
 FAR = ((-2, 0), (2, 0), (0, -2), (0, 2), (-1, -1), (-1, 1), (1, -1), (1, 1))
 AROUND = NEAR + FAR
+ORDER = (0, 2, 1, 3, 0)
+FIRST = {(-1, -1): 0, (1, -1): 1, (1, 1): 2, (-1, 1): 3, (-2, 0): 0, (0, -2): 1, (2, 0): 2, (0, 2): 3}
 
 
 def take_lanes(values, lanes):
@@ -38,10 +40,10 @@
     out_vel, out_imp,
     vel_ref, mass_ref, drag_ref, cell_ref, bound_ref, pair_ref, frame_ref, block_ref,
     start_ref, gap_ref, mask_ref, pres_raw, pres_wide, pres_ref,
-    pres_in, grain_in, grain_out, ghost_in, sum_in, ghost_out, sum_out,
+    pres_in, grain_in, grain_out, ghost_in, sum_in, far_in, ghost_out, sum_out,
     slope_s, slope_n, vel_s, free_s, stage, ends, codes, lanes_s, spots, table, ext, ghost_s,
-    left, sums, ghost_sums, bound_hot, bound_row,
-    send_sem, recv_sem, pres_send, pres_recv, load_sem,
+    left, sums, ghost_sums, bound_hot, bound_row, part_s, same, split, joined,
+    send_sem, recv_sem, pres_send, pres_recv, far_send, far_recv, load_sem,
 ):
     nx, ny = sizes
     tiles = mask_ref.shape[0]
@@ -129,7 +131,7 @@
     upper = row_iota < side_rows
     low_at = two_at < half
 
-    def pick(row_of, kinds):
+    def pick(row_of, kinds, unroll):
         def body(k, acc):
             acc = list(acc)
             for i in range(4):
@@ -141,7 +143,7 @@
             return tuple(acc)
 
         start = tuple(jnp.zeros((8, LANES), kind) for kind in kinds)
-        acc = lax.fori_loop(0, half // 4, body, start, unroll=2)
+        acc = lax.fori_loop(0, half // 4, body, start, unroll=unroll)
         return [
             jnp.where(low_at[:side_rows], got[:side_rows], got[side_rows:]) for got in acc
         ]
@@ -152,12 +154,14 @@
             return jnp.broadcast_to(vel_ref[pl.ds(c, 1), cols], (8, LANES))
         return spread_row((drag_ref, mass_ref, cell_ref)[c - 3], r)
 
-    *moving, drag_b, mass_b, cell_b = pick(grain_row, (F32,) * 5 + (jnp.int32,))
+    *moving, drag_b, mass_b, cell_b = pick(grain_row, (F32,) * 5 + (jnp.int32,), 2)
     below = 1.0 + TIME_STEP * drag_b
     for c in range(3):
         grain_out[c * side_rows : (c + 1) * side_rows, :] = moving[c] / below
     grain_out[3 * side_rows : 4 * side_rows, :] = TIME_STEP * (drag_b + mass_b) / below
     grain_out[4 * side_rows : 5 * side_rows, :] = cell_b.astype(F32)
+    grain_out[5 * side_rows : 6 * side_rows, :] = mass_b
+    grain_out[6 * side_rows : 7 * side_rows, :] = bound_all.astype(F32)
     pl.semaphore_wait(barrier, len(others))
     spreading = {}
     for k in others:
@@ -218,11 +222,6 @@
         cols = slice(q * LANES, (q + 1) * LANES)
         bound_hot[:, cols] = jnp.where(hot_iota == bound_lane[q : q + 1], 1.0, 0.0).astype(BF16)
         bound_row[:, cols] = jnp.where(row_hot == bound_at[q : q + 1], 1.0, 0.0).astype(BF16)
-
-    def pick_bound(turn):
-        got = pick(lambda c, r: spread_row(ext, c * ext_rows + 2 * r), (F32,) * 3)
-        for c in range(3):
-            ghost_out[turn, c * side_rows : (c + 1) * side_rows, :] = got[c]
 
     def spread_halves(ref, first, value):
         rows = value.shape[0]
@@ -335,6 +334,7 @@
     for c in range(3):
         spread_halves(ghost_s, c * gpad, jnp.concatenate(ghost_free[c], axis=0))
 
+    split[...] = jnp.zeros(split.shape, F32)
     nt = (((1,), (1,)), ((), ()))
     for sweep in range(SWEEPS):
         def contacts(u, odd):
@@ -458,10 +458,32 @@
                 terms = [(h, h * 6 + c * 2) for h in range(2)]
                 total = gather_halves(ghost_sums, ghost_part, GHOST_PITCH, 1, r, terms)
                 for i in range(0, 8, side_rows):
-                    sum_out[
-                        sweep, (r + i) // side_rows, c * side_rows : (c + 1) * side_rows, :
-                    ] = total[i : i + side_rows]
-        flying = exchange(1 + 2 * sweep, lambda g: sum_out.at[sweep, g], lambda g: sum_in.at[sweep, g])
+                    for slot, group in enumerate(ORDER):
+                        if group == (r + i) // side_rows:
+                            sum_out[sweep, slot, c * side_rows : (c + 1) * side_rows, :] = total[
+                                i : i + side_rows
+                            ]
+        flying = exchange(
+            1 + 2 * sweep,
+            lambda g: sum_out.at[sweep, ORDER.index(g)],
+            lambda g: sum_in.at[sweep, g],
+        )
+        distant = {}
+        if sweep < SWEEPS - 1:
+            for k in others[4:]:
+                dx, dy = AROUND[k]
+                back = AROUND.index((-dx, -dy))
+                count = 1 if k < 8 else 2
+                distant[back] = pltpu.make_async_remote_copy(
+                    src_ref=sum_out.at[sweep, pl.ds(FIRST[dx, dy], count)],
+                    dst_ref=far_in.at[sweep, back - 4, pl.ds(0, count)],
+                    send_sem=far_send.at[sweep, k - 4],
+                    recv_sem=far_recv.at[sweep, back - 4],
+                    device_id=reach(dx, dy),
+                    device_id_type=pl.DeviceIdType.MESH,
+                )
+            for copy in distant.values():
+                copy.start()
         own_total = []
         for c in range(3):
             parts = []
@@ -469,6 +491,26 @@
                 terms = [(h, h * 6 + c * 2) for h in range(4)]
                 parts.append(gather_halves(sums, own_part, OWN_PITCH, 2, r, terms))
             own_total.append(jnp.concatenate(parts, axis=0))
+        mass = mass_ref[...]
+        for c in range(3):
+            rows = slice(c * own_rows, (c + 1) * own_rows)
+            part_s[rows, :] = free_s[rows, :] + mass * own_total[c]
+        if sweep < SWEEPS - 1:
+            got = pick(lambda c, r: spread_row(part_s, c * own_rows + r), (F32,) * 3, 4)
+            for c in range(3):
+                ghost_out[sweep, c * side_rows : (c + 1) * side_rows, :] = got[c]
+            bases = exchange(
+                2 + 2 * sweep, lambda g: ghost_out.at[sweep], lambda g: ghost_in.at[sweep, g]
+            )
+            if sweep == 0:
+                for g in range(4):
+                    list_in = grain_in[g, 6 * side_rows : 7 * side_rows, :]
+                    for a in range(side_rows):
+                        down = jnp.broadcast_to(list_in[a : a + 1], (LANES, LANES)).T
+                        for b in range(side_rows):
+                            same[g, b, a * LANES : (a + 1) * LANES, :] = jnp.where(
+                                down == list_in[b : b + 1], 1.0, 0.0
+                            ).astype(BF16)
         if sweep == SWEEPS - 1:
 
             def unstage(t, carry):
@@ -485,9 +527,8 @@
         )
         high = received.astype(BF16).astype(F32)
         low = received - high
-        mass = mass_ref[...]
         for c in range(3):
-            total = own_total[c]
+            total = None
             for term in (high, low):
                 row = jnp.concatenate(
                     [
@@ -499,32 +540,56 @@
                     ],
                     axis=1,
                 )
-                total = total + lax.dot_general(
-                    row, bound_hot[...], nt, preferred_element_type=F32
-                )
-            current = free_s[c * own_rows : (c + 1) * own_rows, :] + mass * total
+                got = lax.dot_general(row, bound_hot[...], nt, preferred_element_type=F32)
+                total = got if total is None else total + got
+            current = part_s[c * own_rows : (c + 1) * own_rows, :] + mass * total
             if sweep < SWEEPS - 1:
                 spread_current(c, current)
             else:
                 vel_s[pl.ds(c, own_rows, stride=3), :] = current
         if sweep < SWEEPS - 1:
-            pick_bound(sweep)
-            flying = exchange(
-                2 + 2 * sweep, lambda g: ghost_out.at[sweep], lambda g: ghost_in.at[sweep, g]
-            )
-            finish(flying)
+            for copy in distant.values():
+                copy.wait_recv()
+            sent.extend(distant.values())
+
+            def sum_of(dx, dy, group):
+                if dx % nx == 0 and dy % ny == 0:
+                    return sum_out[sweep, ORDER.index(group)]
+                at = AROUND.index((dx, dy)) - 4
+                return far_in[sweep, at, int(ORDER[FIRST[-dx, -dy]] != group)]
+
+            for g in range(4):
+                total = None
+                for d in range(4):
+                    dx, dy = NEAR[g][0] + NEAR[d][0], NEAR[g][1] + NEAR[d][1]
+                    got = sum_of(dx, dy, d ^ 1)
+                    total = got if total is None else total + got
+                high = total.astype(BF16).astype(F32)
+                split[g, 0 : 3 * side_rows, :] = high
+                split[g, 3 * side_rows : 6 * side_rows, :] = total - high
+                rows = jnp.concatenate(
+                    [split[g, pl.ds(q, 16, stride=side_rows), :] for q in range(side_rows)], axis=1
+                ).astype(BF16)
+                got = jnp.dot(
+                    rows,
+                    jnp.concatenate([same[g, q] for q in range(side_rows)], axis=1),
+                    preferred_element_type=F32,
+                )
+                for q in range(side_rows):
+                    joined[g, q * 9 : q * 9 + 8, :] = got[0:8, q * LANES : (q + 1) * LANES]
+            finish(bases)
             for c in range(3):
-                spread_halves(
-                    ghost_s,
-                    c * gpad,
-                    jnp.concatenate(
-                        [
-                            ghost_in[sweep, g, c * side_rows : (c + 1) * side_rows, :]
-                            for g in range(4)
-                        ],
-                        axis=0,
-                    ),
-                )
+                ghosts = []
+                for g in range(4):
+                    more = (
+                        joined[g, pl.ds(c, side_rows, stride=9), :]
+                        + joined[g, pl.ds(3 + c, side_rows, stride=9), :]
+                    )
+                    ghosts.append(
+                        ghost_in[sweep, g, c * side_rows : (c + 1) * side_rows, :]
+                        + grain_in[g, 5 * side_rows : 6 * side_rows, :] * more
+                    )
+                spread_halves(ghost_s, c * gpad, jnp.concatenate(ghosts, axis=0))
 
     def unstage_grain(t, carry):
         cols = pl.ds(pl.multiple_of(t * LANES, LANES), LANES)
@@ -590,12 +655,13 @@
                 pltpu.VMEM((pressure.size // pressure.shape[2], LANES), F32),
                 pltpu.VMEM((cell_rows, LANES), F32),
                 pltpu.VMEM((12, cell_rows, LANES), F32),
-                pltpu.VMEM((4, 5 * side_rows, LANES), F32),
-                pltpu.VMEM((5 * side_rows, LANES), F32),
+                pltpu.VMEM((4, 7 * side_rows, LANES), F32),
+                pltpu.VMEM((7 * side_rows, LANES), F32),
                 pltpu.VMEM((SWEEPS - 1, 4, 3 * side_rows, LANES), F32),
                 pltpu.VMEM((SWEEPS, 4, 3 * side_rows, LANES), F32),
+                pltpu.VMEM((SWEEPS - 1, 8, 2, 3 * side_rows, LANES), F32),
                 pltpu.VMEM((SWEEPS - 1, 3 * side_rows, LANES), F32),
-                pltpu.VMEM((SWEEPS, 4, 3 * side_rows, LANES), F32),
+                pltpu.VMEM((SWEEPS, 5, 3 * side_rows, LANES), F32),
                 pltpu.VMEM((3 * cell_rows, LANES), F32),
                 pltpu.VMEM((12 * cell_rows, LANES), F32),
                 pltpu.VMEM((own_rows * 3, LANES), F32),
@@ -613,10 +679,16 @@
                 pltpu.VMEM((2 * (4 * side_rows + 1) * GHOST_PITCH, LANES), F32),
                 pltpu.VMEM((LANES, side_rows * LANES), BF16),
                 pltpu.VMEM((own_rows, side_rows * LANES), BF16),
+                pltpu.VMEM((3 * own_rows, LANES), F32),
+                pltpu.VMEM((4, side_rows, side_rows * LANES, LANES), BF16),
+                pltpu.VMEM((4, 16 * side_rows, LANES), F32),
+                pltpu.VMEM((4, 9 * side_rows, LANES), F32),
                 pltpu.SemaphoreType.DMA((rounds, 4)),
                 pltpu.SemaphoreType.DMA((rounds, 4)),
                 pltpu.SemaphoreType.DMA((12,)),
                 pltpu.SemaphoreType.DMA((12,)),
+                pltpu.SemaphoreType.DMA((SWEEPS - 1, 8)),
+                pltpu.SemaphoreType.DMA((SWEEPS - 1, 8)),
                 pltpu.SemaphoreType.DMA((12,)),
             ],
             compiler_params=pltpu.CompilerParams(

time: 32.2 us -> 28.5 us (0.89)
  Pallas kernels: 31.4 us -> 27.7 us
    pallas_call x1, Pallas kernels: 29.7 us -> 25.9 us  [local(): pl.pallas_call(lambda *refs: step_kernel(sizes, *refs), out_shape=(jax.Sh...]
where the time goes in v3:
time: 28.5 us; the launch traced here: 28.3 us
  Pallas kernels  27.7 us (97%)
  between operations  0.64 us (2%)
    pallas_call x1, Pallas kernels, local(): pl.pallas_call(lambda *refs: step_kernel(sizes, *refs), out_shape=(jax.Sh...  25.9 us
    pallas_call x1, Pallas kernels, local(): pl.pallas_call(hand_on, out_shape=(jax.ShapeDtypeStruct(velocity.shape, F...  1.73 us

profile of v3, /device:TPU:0, one launch (start us, length us, event | category | flops | bytes accessed | tf_op | source)
XLA Modules:
  0.0 28.3 jit_solution(6521784294815065794)
XLA Ops:
  0.6 25.9 %shard_map.131 = (f32[3,8192]{1,0:T(4,128)}, f32[3,16384]{1,0:T(4,128)}) custom-call(f32[3,8192]{1,0:T(4,128)} %refs_0_.1, f32[64,128]{1,0:T(8,128)} %bitcast.6, f32[64,128]{1,0:T(8,128)} %bitcast.7, s32[64,128]{1,0:T(8,128)} %bitcast.8, s32[4,128]{1,0:T(4,128)} %bitcast.9, s32[2,16384]{1,0:T(2,128)} %refs_5_.1, f32[9,16384]{1,0:T(8,128)} %refs_6_.1, ...), custom_call_target="tpu_custom_call" | custom-call | tf_op jit(solution)/shard_map/pallas_call | solution.py:634
  26.6 1.7 %shard_map.132 = (f32[3,8192]{1,0:T(4,128)}, f32[3,16384]{1,0:T(4,128)}) custom-call(f32[3,8192]{1,0:T(4,128)} %get-tuple-element.4.vel_in, f32[3,16384]{1,0:T(4,128)} %get-tuple-element.5.imp_in), custom_call_target="tpu_custom_call" | custom-call | tf_op jit(solution)/shard_map/pallas_call | solution.py:711

commit v4 on v3

--- a/solution.py
+++ b/solution.py
@@ -515,12 +515,10 @@
 
             def unstage(t, carry):
                 cols = pl.ds(pl.multiple_of(t * LANES, LANES), LANES)
-                start_ref[:, cols] = stage[pl.ds(t * STAGE + 32, 3), :]
+                out_imp[:, cols] = stage[pl.ds(t * STAGE + 32, 3), :]
                 return carry
 
             lax.fori_loop(0, tiles, unstage, 0, unroll=8)
-            imp_store = pltpu.make_async_copy(start_ref, out_imp, load_sem.at[0])
-            imp_store.start()
         finish(flying)
         received = (
             sum_in[sweep, 0] + sum_in[sweep, 1] + sum_in[sweep, 2] + sum_in[sweep, 3]
@@ -593,29 +591,23 @@
 
     def unstage_grain(t, carry):
         cols = pl.ds(pl.multiple_of(t * LANES, LANES), LANES)
-        vel_ref[:, cols] = vel_s[pl.ds(t * 3, 3), :]
+        out_vel[:, cols] = vel_s[pl.ds(t * 3, 3), :]
         return carry
 
     lax.fori_loop(0, own_rows, unstage_grain, 0, unroll=8)
-    vel_store = pltpu.make_async_copy(vel_ref, out_vel, load_sem.at[1])
-    vel_store.start()
     for copy in sent:
         copy.wait_send()
-    imp_store.wait()
-    vel_store.wait()
-
-
-def hand_on(vel_in, imp_in, vel_out, imp_out, vel_ref, imp_ref, sem):
-    pairs = ((imp_in, imp_ref, imp_out), (vel_in, vel_ref, vel_out))
-    loads = [pltpu.make_async_copy(x, y, sem.at[0, k]) for k, (x, y, _) in enumerate(pairs)]
-    stores = [pltpu.make_async_copy(y, z, sem.at[1, k]) for k, (_, y, z) in enumerate(pairs)]
-    for load in loads:
-        load.start()
-    for load, store in zip(loads, stores):
-        load.wait()
-        store.start()
-    for store in stores:
-        store.wait()
+
+
+def hand_on(vel_in, imp_in, vel_out, imp_out, sem):
+    copies = [
+        pltpu.make_async_copy(imp_in, imp_out, sem.at[0]),
+        pltpu.make_async_copy(vel_in, vel_out, sem.at[1]),
+    ]
+    for copy in copies:
+        copy.start()
+    for copy in copies:
+        copy.wait()
 
 
 def solution(mesh):
@@ -633,12 +625,9 @@
         rounds = 2 * SWEEPS
         out_vel, out_imp = pl.pallas_call(
             lambda *refs: step_kernel(sizes, *refs),
-            out_shape=(
-                jax.ShapeDtypeStruct(velocity.shape, F32),
-                jax.ShapeDtypeStruct(impulse_start.shape, F32),
-            ),
+            out_shape=(pltpu.VMEM(velocity.shape, F32), pltpu.VMEM(impulse_start.shape, F32)),
             in_specs=[pl.BlockSpec(memory_space=pltpu.HBM)] * 12,
-            out_specs=(pl.BlockSpec(memory_space=pltpu.HBM),) * 2,
+            out_specs=(pl.BlockSpec(memory_space=pltpu.VMEM),) * 2,
             scratch_shapes=[
                 pltpu.VMEM((3, velocity.shape[1]), F32),
                 pltpu.VMEM((own_rows, LANES), F32),
@@ -692,7 +681,7 @@
                 pltpu.SemaphoreType.DMA((12,)),
             ],
             compiler_params=pltpu.CompilerParams(
-                collective_id=0, has_side_effects=True, vmem_limit_bytes=62 * 1024 * 1024
+                collective_id=0, has_side_effects=True, vmem_limit_bytes=60 * 1024 * 1024
             ),
         )(
             velocity,
@@ -714,14 +703,13 @@
                 jax.ShapeDtypeStruct(velocity.shape, F32),
                 jax.ShapeDtypeStruct(impulse_start.shape, F32),
             ),
-            in_specs=[pl.BlockSpec(memory_space=pltpu.HBM)] * 2,
+            in_specs=[pl.BlockSpec(memory_space=pl.ANY)] * 2,
             out_specs=(pl.BlockSpec(memory_space=pltpu.HBM),) * 2,
-            scratch_shapes=[
-                pltpu.VMEM(velocity.shape, F32),
-                pltpu.VMEM(impulse_start.shape, F32),
-                pltpu.SemaphoreType.DMA((2, 2)),
-            ],
-        )(out_vel, out_imp)
+            scratch_shapes=[pltpu.SemaphoreType.DMA((2,))],
+        )(
+            pltpu.with_memory_space_constraint(out_vel, pltpu.VMEM),
+            pltpu.with_memory_space_constraint(out_imp, pltpu.VMEM),
+        )
 
     grains, lists = P(("gx", "gy")), P(None, ("gx", "gy"))
     return jax.shard_map(

time: 28.5 us -> 26.9 us (0.944)
  Pallas kernels: 27.7 us -> 26.1 us
    pallas_call x1, Pallas kernels: 1.73 us -> 0.76 us  [local(): pl.pallas_call(hand_on, out_shape=(jax.ShapeDtypeStruct(velocity.shape, F...]
    pallas_call x1, Pallas kernels: 25.9 us -> 25.3 us  [local(): pl.pallas_call(lambda *refs: step_kernel(sizes, *refs), out_shape=(pltpu....]
where the time goes in v4:
time: 26.9 us; the launch traced here: 26.7 us
  Pallas kernels  26.1 us (97%)
  between operations  0.64 us (2%)
    pallas_call x1, Pallas kernels, local(): pl.pallas_call(lambda *refs: step_kernel(sizes, *refs), out_shape=(pltpu....  25.3 us
    pallas_call x1, Pallas kernels, local(): pl.pallas_call(hand_on, out_shape=(jax.ShapeDtypeStruct(velocity.shape, F...  0.76 us

profile of v4, /device:TPU:0, one launch (start us, length us, event | category | flops | bytes accessed | tf_op | source)
XLA Modules:
  0.0 26.7 jit_solution(3964966911416473525)
XLA Ops:
  0.6 25.3 %shard_map.131 = (f32[3,8192]{1,0:T(4,128)S(1)}, f32[3,16384]{1,0:T(4,128)S(1)}) custom-call(f32[3,8192]{1,0:T(4,128)} %refs_0_.1, f32[64,128]{1,0:T(8,128)} %bitcast.6, f32[64,128]{1,0:T(8,128)} %bitcast.7, s32[64,128]{1,0:T(8,128)} %bitcast.8, s32[4,128]{1,0:T(4,128)} %bitcast.9, s32[2,16384]{1,0:T(2,128)} %refs_5_.1, f32[9,16384]{1,0:T(8,128)} %refs_6_.1, ...), custom_call_target="tpu_custom_call" | custom-call | tf_op jit(solution)/shard_map/pallas_call | solution.py:626
  26.0 0.8 %shard_map.132 = (f32[3,8192]{1,0:T(4,128)}, f32[3,16384]{1,0:T(4,128)}) custom-call(f32[3,8192]{1,0:T(4,128)S(1)} %get-tuple-element.4.vel_in, f32[3,16384]{1,0:T(4,128)S(1)} %get-tuple-element.5.imp_in), custom_call_target="tpu_custom_call" | custom-call | tf_op jit(solution)/shard_map/pallas_call | solution.py:700

commit v5 on v4

--- a/solution.py
+++ b/solution.py
@@ -42,7 +42,7 @@
     start_ref, gap_ref, mask_ref, pres_raw, pres_wide, pres_ref,
     pres_in, grain_in, grain_out, ghost_in, sum_in, far_in, ghost_out, sum_out,
     slope_s, slope_n, vel_s, free_s, stage, ends, codes, lanes_s, spots, table, ext, ghost_s,
-    left, sums, ghost_sums, bound_hot, bound_row, part_s, same, split, joined,
+    left, sums, ghost_sums, bound_hot, bound_row, part_s, push_s, same, split, joined,
     send_sem, recv_sem, pres_send, pres_recv, far_send, far_recv, load_sem,
 ):
     nx, ny = sizes
@@ -251,7 +251,7 @@
         return carry
 
     lax.fori_loop(0, tiles, build, 0, unroll=4)
-    for i in range(32):
+    for i in range(64):
         left[i * PITCH + 36 : i * PITCH + ROWS, :] = jnp.zeros((12, LANES), F32)
 
     for k in range(4):
@@ -387,22 +387,31 @@
             imp = [normal * active, factor * trial[1] * active, factor * trial[2] * active]
             for k in range(3):
                 stage[pl.ds(u * (8 * STAGE) + 32 + k, 8, stride=STAGE), :] = imp[k]
+            pushes = [fr[c] * imp[0] + fr[3 + c] * imp[1] + fr[6 + c] * imp[2] for c in range(3)]
+            if sweep < SWEEPS - 1:
+                scatter(u, odd, code, pushes, range(6))
+                return
             for c in range(3):
-                push = fr[c] * imp[0] + fr[3 + c] * imp[1] + fr[6 + c] * imp[2]
-                high = push.astype(BF16).astype(F32)
-                for s, term in enumerate((high, push - high)):
+                push_s[c, at, :] = pushes[c]
+            scatter(u, odd, code, pushes, (4, 5))
+
+        def scatter(u, odd, code, pushes, blocks):
+            rows = -(-len(blocks) * 6 // 16) * 16
+            for c in range(3):
+                high = pushes[c].astype(BF16).astype(F32)
+                for s, term in enumerate((high, pushes[c] - high)):
                     for e in range(2):
-                        for h in range(6):
+                        for n, h in enumerate(blocks):
                             left[
-                                pl.ds((e * 8 + odd) * PITCH + (h * 3 + c) * 2 + s, 8, stride=PITCH), :
+                                pl.ds((e * 8 + odd) * PITCH + (n * 3 + c) * 2 + s, 8, stride=PITCH), :
                             ] = jnp.where(code[e] == h, term, 0.0)
             ghost_sum = None
             for i in range(8):
                 got = lax.dot_general(
                     jnp.concatenate(
                         [
-                            left[(odd + i) * PITCH : (odd + i) * PITCH + ROWS, :].astype(BF16),
-                            left[(odd + i + 8) * PITCH : (odd + i + 8) * PITCH + ROWS, :].astype(BF16),
+                            left[first : first + rows, :].astype(BF16)
+                            for first in ((odd + i) * PITCH, (odd + i + 8) * PITCH)
                         ],
                         axis=1,
                     ),
@@ -416,27 +425,37 @@
                     nt,
                     preferred_element_type=F32,
                 )
-                at = ((i & 1) * own_part + u * 4 + (i >> 1) + 2) * OWN_PITCH
-                sums[pl.ds(at, 24), 0:HALF] = got[0:24]
-                ghost_sum = got[24:40] if i % 4 == 0 else ghost_sum + got[24:40]
-                if i % 4 == 3:
-                    at = ((i >> 2) * ghost_part + u + 1) * GHOST_PITCH
-                    ghost_sums[pl.ds(at, 16), 0:HALF] = ghost_sum
+                if 0 in blocks:
+                    at = ((i & 1) * own_part + u * 4 + (i >> 1) + 2) * OWN_PITCH
+                    sums[pl.ds(at, 24), 0:HALF] = got[0:24]
+                if 5 in blocks:
+                    far = 6 * (len(blocks) - 2)
+                    got = got[far : far + 16]
+                    ghost_sum = got if i % 4 == 0 else ghost_sum + got
+                    if i % 4 == 3:
+                        at = ((i >> 2) * ghost_part + u + 1) * GHOST_PITCH
+                        ghost_sums[pl.ds(at, 16), 0:HALF] = ghost_sum
+
+        def own_scatter(u, odd):
+            at = pl.ds(pl.multiple_of(u * 8, 8), 8)
+            code = [codes[pl.ds(pl.multiple_of(e * tiles + u * 8, 8), 8), :] for e in range(2)]
+            scatter(u, odd, code, [push_s[c, at, :] for c in range(3)], range(4))
+
+        def own_two(k, carry):
+            for i in range(4):
+                own_scatter(4 * k + i, 16 * i)
+            return carry
 
         def two(k, carry):
-            contacts(2 * k, 0)
-            contacts(2 * k + 1, 16)
+            for i in range(4):
+                contacts(4 * k + i, 16 * i)
             return carry
 
-        lax.fori_loop(0, tiles // 16, two, 0, unroll=2)
+        lax.fori_loop(0, tiles // 32, two, 0, unroll=4)
         for par in range(2):
             base = par * ghost_part * GHOST_PITCH
             ghost_sums[base : base + GHOST_PITCH, :] = ghost_sums[
                 base + ghost_rows * GHOST_PITCH : base + (ghost_rows + 1) * GHOST_PITCH, :
-            ]
-            base = par * own_part * OWN_PITCH
-            sums[base : base + 2 * OWN_PITCH, :] = sums[
-                base + own_rows * OWN_PITCH : base + (own_rows + 2) * OWN_PITCH, :
             ]
         first_half = lax.broadcasted_iota(jnp.int32, (8, LANES), 1) < HALF
 
@@ -484,6 +503,13 @@
                 )
             for copy in distant.values():
                 copy.start()
+        if sweep == SWEEPS - 1:
+            lax.fori_loop(0, tiles // 32, own_two, 0, unroll=2)
+        for par in range(2):
+            base = par * own_part * OWN_PITCH
+            sums[base : base + 2 * OWN_PITCH, :] = sums[
+                base + own_rows * OWN_PITCH : base + (own_rows + 2) * OWN_PITCH, :
+            ]
         own_total = []
         for c in range(3):
             parts = []
@@ -663,12 +689,13 @@
                 pltpu.VMEM((tiles, LANES, LANES), BF16),
                 pltpu.VMEM((3 * (2 * own_rows + 8), LANES), F32),
                 pltpu.VMEM((3 * gpad, LANES), F32),
-                pltpu.VMEM((32 * PITCH, LANES), F32),
+                pltpu.VMEM((64 * PITCH, LANES), F32),
                 pltpu.VMEM((2 * (own_rows + 2) * OWN_PITCH, LANES), F32),
                 pltpu.VMEM((2 * (4 * side_rows + 1) * GHOST_PITCH, LANES), F32),
                 pltpu.VMEM((LANES, side_rows * LANES), BF16),
                 pltpu.VMEM((own_rows, side_rows * LANES), BF16),
                 pltpu.VMEM((3 * own_rows, LANES), F32),
+                pltpu.VMEM((3, tiles, LANES), F32),
                 pltpu.VMEM((4, side_rows, side_rows * LANES, LANES), BF16),
                 pltpu.VMEM((4, 16 * side_rows, LANES), F32),
                 pltpu.VMEM((4, 9 * side_rows, LANES), F32),

time: 26.9 us -> 25.2 us (0.937)
  Pallas kernels: 26.1 us -> 24.4 us
    pallas_call x1, Pallas kernels: 25.3 us -> 23.7 us  [local(): pl.pallas_call(lambda *refs: step_kernel(sizes, *refs), out_shape=(pltpu....]
where the time goes in v5:
time: 25.2 us; the launch traced here: 25.1 us
  Pallas kernels  24.4 us (97%)
  between operations  0.64 us (3%)
    pallas_call x1, Pallas kernels, local(): pl.pallas_call(lambda *refs: step_kernel(sizes, *refs), out_shape=(pltpu....  23.7 us
    pallas_call x1, Pallas kernels, local(): pl.pallas_call(hand_on, out_shape=(jax.ShapeDtypeStruct(velocity.shape, F...  0.76 us

profile of v5, /device:TPU:0, one launch (start us, length us, event | category | flops | bytes accessed | tf_op | source)
XLA Modules:
  0.0 25.1 jit_solution(50636914362605262)
XLA Ops:
  0.6 23.7 %shard_map.131 = (f32[3,8192]{1,0:T(4,128)S(1)}, f32[3,16384]{1,0:T(4,128)S(1)}) custom-call(f32[3,8192]{1,0:T(4,128)} %refs_0_.1, f32[64,128]{1,0:T(8,128)} %bitcast.6, f32[64,128]{1,0:T(8,128)} %bitcast.7, s32[64,128]{1,0:T(8,128)} %bitcast.8, s32[4,128]{1,0:T(4,128)} %bitcast.9, s32[2,16384]{1,0:T(2,128)} %refs_5_.1, f32[9,16384]{1,0:T(8,128)} %refs_6_.1, ...), custom_call_target="tpu_custom_call" | custom-call | tf_op jit(solution)/shard_map/pallas_call | solution.py:652
  24.3 0.8 %shard_map.132 = (f32[3,8192]{1,0:T(4,128)}, f32[3,16384]{1,0:T(4,128)}) custom-call(f32[3,8192]{1,0:T(4,128)S(1)} %get-tuple-element.4.vel_in, f32[3,16384]{1,0:T(4,128)S(1)} %get-tuple-element.5.imp_in), custom_call_target="tpu_custom_call" | custom-call | tf_op jit(solution)/shard_map/pallas_call | solution.py:727

commit v6 on v5

--- a/solution.py
+++ b/solution.py
@@ -154,7 +154,7 @@
             return jnp.broadcast_to(vel_ref[pl.ds(c, 1), cols], (8, LANES))
         return spread_row((drag_ref, mass_ref, cell_ref)[c - 3], r)
 
-    *moving, drag_b, mass_b, cell_b = pick(grain_row, (F32,) * 5 + (jnp.int32,), 2)
+    *moving, drag_b, mass_b, cell_b = pick(grain_row, (F32,) * 5 + (jnp.int32,), 8)
     below = 1.0 + TIME_STEP * drag_b
     for c in range(3):
         grain_out[c * side_rows : (c + 1) * side_rows, :] = moving[c] / below
@@ -301,7 +301,7 @@
             ) / (1.0 + TIME_STEP * drag)
         return carry
 
-    lax.fori_loop(0, own_rows // 8, free, 0, unroll=2)
+    lax.fori_loop(0, own_rows // 8, free, 0, unroll=8)
     for c in range(3):
         spread_current(c, free_s[c * own_rows : (c + 1) * own_rows, :])
     for k in others[4:]:
@@ -522,7 +522,7 @@
             rows = slice(c * own_rows, (c + 1) * own_rows)
             part_s[rows, :] = free_s[rows, :] + mass * own_total[c]
         if sweep < SWEEPS - 1:
-            got = pick(lambda c, r: spread_row(part_s, c * own_rows + r), (F32,) * 3, 4)
+            got = pick(lambda c, r: spread_row(part_s, c * own_rows + r), (F32,) * 3, 8)
             for c in range(3):
                 ghost_out[sweep, c * side_rows : (c + 1) * side_rows, :] = got[c]
             bases = exchange(
@@ -551,21 +551,26 @@
         )
         high = received.astype(BF16).astype(F32)
         low = received - high
+        rows = [
+            jnp.concatenate(
+                [
+                    bound_row[:, q * LANES : (q + 1) * LANES]
+                    * jnp.broadcast_to(
+                        term[c * side_rows + q : c * side_rows + q + 1], (own_rows, LANES)
+                    ).astype(BF16)
+                    for q in range(side_rows)
+                ],
+                axis=1,
+            )
+            for c in range(3)
+            for term in (high, low)
+        ]
+        got = lax.dot_general(
+            jnp.concatenate(rows, axis=0), bound_hot[...], nt, preferred_element_type=F32
+        )
         for c in range(3):
-            total = None
-            for term in (high, low):
-                row = jnp.concatenate(
-                    [
-                        bound_row[:, q * LANES : (q + 1) * LANES]
-                        * jnp.broadcast_to(
-                            term[c * side_rows + q : c * side_rows + q + 1], (own_rows, LANES)
-                        ).astype(BF16)
-                        for q in range(side_rows)
-                    ],
-                    axis=1,
-                )
-                got = lax.dot_general(row, bound_hot[...], nt, preferred_element_type=F32)
-                total = got if total is None else total + got
+            first = 2 * c * own_rows
+            total = got[first : first + own_rows] + got[first + own_rows : first + 2 * own_rows]
             current = part_s[c * own_rows : (c + 1) * own_rows, :] + mass * total
             if sweep < SWEEPS - 1:
                 spread_current(c, current)

time: 25.2 us -> 25 us (level)
  no operation moved by 1% of the time
where the time goes in v6:
time: 25 us; the launch traced here: 24.8 us
  Pallas kernels  24.2 us (97%)
  between operations  0.64 us (3%)
    pallas_call x1, Pallas kernels, local(): pl.pallas_call(lambda *refs: step_kernel(sizes, *refs), out_shape=(pltpu....  23.4 us
    pallas_call x1, Pallas kernels, local(): pl.pallas_call(hand_on, out_shape=(jax.ShapeDtypeStruct(velocity.shape, F...  0.76 us

profile of v6, /device:TPU:0, one launch (start us, length us, event | category | flops | bytes accessed | tf_op | source)
XLA Modules:
  0.0 24.8 jit_solution(1141696785321261354)
XLA Ops:
  0.6 23.4 %shard_map.131 = (f32[3,8192]{1,0:T(4,128)S(1)}, f32[3,16384]{1,0:T(4,128)S(1)}) custom-call(f32[3,8192]{1,0:T(4,128)} %refs_0_.1, f32[64,128]{1,0:T(8,128)} %bitcast.6, f32[64,128]{1,0:T(8,128)} %bitcast.7, s32[64,128]{1,0:T(8,128)} %bitcast.8, s32[4,128]{1,0:T(4,128)} %bitcast.9, s32[2,16384]{1,0:T(2,128)} %refs_5_.1, f32[9,16384]{1,0:T(8,128)} %refs_6_.1, ...), custom_call_target="tpu_custom_call" | custom-call | tf_op jit(solution)/shard_map/pallas_call | solution.py:657
  24.1 0.8 %shard_map.132 = (f32[3,8192]{1,0:T(4,128)}, f32[3,16384]{1,0:T(4,128)}) custom-call(f32[3,8192]{1,0:T(4,128)S(1)} %get-tuple-element.4.vel_in, f32[3,16384]{1,0:T(4,128)S(1)} %get-tuple-element.5.imp_in), custom_call_target="tpu_custom_call" | custom-call | tf_op jit(solution)/shard_map/pallas_call | solution.py:732

commit v7 on v6

--- a/solution.py
+++ b/solution.py
@@ -254,8 +254,6 @@
     for i in range(64):
         left[i * PITCH + 36 : i * PITCH + ROWS, :] = jnp.zeros((12, LANES), F32)
 
-    for k in range(4):
-        spreading[k].wait_recv()
     even = (lax.broadcasted_iota(jnp.int32, (cell_rows, LANES), 0) & 1) == 0
     up1 = lambda a: jnp.concatenate([a[1:], a[:1]], axis=0)
     down1 = lambda a: jnp.concatenate([a[-1:], a[:-1]], axis=0)
@@ -267,49 +265,56 @@
             return p
         return pres_in[AROUND.index((dx, dy))]
 
-    def slopes(ref, first, dx, dy):
+    def slope(c, dx, dy):
         mid = pres_at(dx, dy)
-        prev_x, next_x = pres_at(dx - 1, dy), pres_at(dx + 1, dy)
-        prev_y, next_y = pres_at(dx, dy - 1), pres_at(dx, dy + 1)
-        after = turn(mid, -16)
-        plus = jnp.where(lane < 112, after, jnp.where(even, up1(after), down1(turn(next_x, -16))))
-        before = turn(mid, 16)
-        minus = jnp.where(lane >= 16, before, jnp.where(even, up1(turn(prev_x, 16)), down1(before)))
-        ref[first : first + cell_rows] = (plus - minus) * 0.5
-        plus = jnp.where((lane & 15) < 15, turn(mid, -1), turn(next_y, 15))
-        minus = jnp.where((lane & 15) > 0, turn(mid, 1), turn(prev_y, -15))
-        ref[first + cell_rows : first + 2 * cell_rows] = (plus - minus) * 0.5
-        ref[first + 2 * cell_rows : first + 3 * cell_rows] = (
-            jnp.concatenate([mid[2:], none], axis=0) - jnp.concatenate([none, mid[:-2]], axis=0)
-        ) * 0.5
-
-    slopes(slope_s, 0, 0, 0)
-
-    def free(k, carry):
-        at = pl.ds(pl.multiple_of(k * 8, 8), 8)
-        cells = cell_ref[at, :]
-        cell_at, cell_lane = cells >> 7, cells & (LANES - 1)
-        drag, mass = drag_ref[at, :], mass_ref[at, :]
-        for c in range(3):
-            slope = jnp.zeros((8, LANES), F32)
+        if c == 0:
+            prev_x, next_x = pres_at(dx - 1, dy), pres_at(dx + 1, dy)
+            after, before = turn(mid, -16), turn(mid, 16)
+            plus = jnp.where(
+                lane < 112, after, jnp.where(even, up1(after), down1(turn(next_x, -16)))
+            )
+            minus = jnp.where(
+                lane >= 16, before, jnp.where(even, up1(turn(prev_x, 16)), down1(before))
+            )
+        elif c == 1:
+            prev_y, next_y = pres_at(dx, dy - 1), pres_at(dx, dy + 1)
+            plus = jnp.where((lane & 15) < 15, turn(mid, -1), turn(next_y, 15))
+            minus = jnp.where((lane & 15) > 0, turn(mid, 1), turn(prev_y, -15))
+        else:
+            plus = jnp.concatenate([mid[2:], none], axis=0)
+            minus = jnp.concatenate([none, mid[:-2]], axis=0)
+        return (plus - minus) * 0.5
+
+    for c, needs in ((2, ()), (1, (2, 3)), (0, (0, 1))):
+        for k in needs:
+            spreading[k].wait_recv()
+        slope_s[...] = slope(c, 0, 0)
+
+        def free(k, carry):
+            at = pl.ds(pl.multiple_of(k * 8, 8), 8)
+            cells = cell_ref[at, :]
+            cell_at, cell_lane = cells >> 7, cells & (LANES - 1)
+            drag, mass = drag_ref[at, :], mass_ref[at, :]
+            got = jnp.zeros((8, LANES), F32)
             for r in range(cell_rows):
-                got = take_lanes(spread_row(slope_s, c * cell_rows + r), cell_lane)
-                slope = jnp.where(cell_at == r, got, slope)
+                row = take_lanes(spread_row(slope_s, r), cell_lane)
+                got = jnp.where(cell_at == r, row, got)
             v = vel_s[pl.ds(k * 24 + c, 8, stride=3), :]
             free_s[pl.ds(pl.multiple_of(c * own_rows + k * 8, 8), 8), :] = (
-                v - TIME_STEP * (drag + mass) * slope
+                v - TIME_STEP * (drag + mass) * got
             ) / (1.0 + TIME_STEP * drag)
-        return carry
-
-    lax.fori_loop(0, own_rows // 8, free, 0, unroll=8)
-    for c in range(3):
+            return carry
+
+        lax.fori_loop(0, own_rows // 8, free, 0, unroll=8)
         spread_current(c, free_s[c * own_rows : (c + 1) * own_rows, :])
     for k in others[4:]:
         spreading[k].wait_recv()
     sent.extend(spreading.values())
     finish(flying)
     for g in range(4):
-        slopes(slope_n, 3 * cell_rows * g, *NEAR[g])
+        for c in range(3):
+            first = (3 * g + c) * cell_rows
+            slope_n[first : first + cell_rows, :] = slope(c, *NEAR[g])
     ghost_free = [[], [], []]
     for g in (0, 2):
         both = [
@@ -321,7 +326,7 @@
         cells = both[4].astype(jnp.int32)
         cell_at, cell_lane = cells >> 7, cells & (LANES - 1)
         for c in range(3):
-            slope = jnp.zeros((8, LANES), F32)
+            here = jnp.zeros((8, LANES), F32)
             for r in range(cell_rows):
                 first = (3 * g + c) * cell_rows + r
                 row = jnp.where(
@@ -329,8 +334,8 @@
                     spread_row(slope_n, first),
                     spread_row(slope_n, first + 3 * cell_rows),
                 )
-                slope = jnp.where(cell_at == r, take_lanes(row, cell_lane), slope)
-            ghost_free[c].append(both[c] - both[3] * slope)
+                here = jnp.where(cell_at == r, take_lanes(row, cell_lane), here)
+            ghost_free[c].append(both[c] - both[3] * here)
     for c in range(3):
         spread_halves(ghost_s, c * gpad, jnp.concatenate(ghost_free[c], axis=0))
 
@@ -682,7 +687,7 @@
                 pltpu.VMEM((SWEEPS - 1, 8, 2, 3 * side_rows, LANES), F32),
                 pltpu.VMEM((SWEEPS - 1, 3 * side_rows, LANES), F32),
                 pltpu.VMEM((SWEEPS, 5, 3 * side_rows, LANES), F32),
-                pltpu.VMEM((3 * cell_rows, LANES), F32),
+                pltpu.VMEM((cell_rows, LANES), F32),
                 pltpu.VMEM((12 * cell_rows, LANES), F32),
                 pltpu.VMEM((own_rows * 3, LANES), F32),
                 pltpu.VMEM((3 * own_rows, LANES), F32),

time: 25 us -> 25 us (level)
  no operation moved by 1% of the time
where the time goes in v7:
time: 25 us; the launch traced here: 24.9 us
  Pallas kernels  24.2 us (97%)
  between operations  0.64 us (3%)
    pallas_call x1, Pallas kernels, local(): pl.pallas_call(lambda *refs: step_kernel(sizes, *refs), out_shape=(pltpu....  23.5 us
    pallas_call x1, Pallas kernels, local(): pl.pallas_call(hand_on, out_shape=(jax.ShapeDtypeStruct(velocity.shape, F...  0.76 us

profile of v7, /device:TPU:0, one launch (start us, length us, event | category | flops | bytes accessed | tf_op | source)
XLA Modules:
  0.0 24.9 jit_solution(11888763733856925359)
XLA Ops:
  0.6 23.5 %shard_map.131 = (f32[3,8192]{1,0:T(4,128)S(1)}, f32[3,16384]{1,0:T(4,128)S(1)}) custom-call(f32[3,8192]{1,0:T(4,128)} %refs_0_.1, f32[64,128]{1,0:T(8,128)} %bitcast.6, f32[64,128]{1,0:T(8,128)} %bitcast.7, s32[64,128]{1,0:T(8,128)} %bitcast.8, s32[4,128]{1,0:T(4,128)} %bitcast.9, s32[2,16384]{1,0:T(2,128)} %refs_5_.1, f32[9,16384]{1,0:T(8,128)} %refs_6_.1, ...), custom_call_target="tpu_custom_call" | custom-call | tf_op jit(solution)/shard_map/pallas_call | solution.py:662
  24.1 0.8 %shard_map.132 = (f32[3,8192]{1,0:T(4,128)}, f32[3,16384]{1,0:T(4,128)}) custom-call(f32[3,8192]{1,0:T(4,128)S(1)} %get-tuple-element.4.vel_in, f32[3,16384]{1,0:T(4,128)S(1)} %get-tuple-element.5.imp_in), custom_call_target="tpu_custom_call" | custom-call | tf_op jit(solution)/shard_map/pallas_call | solution.py:737
